TPU v7x, 256 devices: a whole 4x4x8 slice. The times are simulated.
256 devices in a mesh: row: 16 (over x, y), col: 16 (over z, core).
Axes of the slice: x: 4, y: 4, z: 8, core: 2. Of those that a mesh axis runs over, the one named last changes fastest.
Arguments:
- factor: float32 [4, 16, 256, 4, 16, 256], P(None, 'row', None, None, 'col'), as said below
- adjoint: float32 [4, 16, 256, 4, 16, 256], P(None, 'row', None, None, 'col'), may hold values from -6 to 6
- diag_inverse: float32 [2, 256, 256], replicated, as said below
Outputs:
- gradient: float32 [4, 16, 256, 4, 16, 256], P(None, 'row', None, None, 'col')
Inputs may be any that keep to these rules, and one draw needn't show every extreme that they name: The diagonal blocks of factor at block indices 32 and 31 are lower triangular with diagonal entries between 1 and 2; diag_inverse[0] and diag_inverse[1] are their inverses. Entries above those blocks' diagonals and above the block diagonal elsewhere are never read. diag_inverse[k] is the inverse of the diagonal block of factor at block index 32 - k.
All inputs are finite; a program needn't handle non-finite values.
Results may differ from a plain program's by a relative error of at most 0.0001.
Values sent between devices are 32-bit elements; how exact they have to be, the bound alone decides.
No kernel may reach another device: no remote copies, remote signals or barrier semaphores. Data moves between devices by JAX's collectives and lax.ppermute only.
A program may use at most 128 MiB of HBM per device.

v0:
```python
import jax
import jax.numpy as jnp
from jax import lax
from jax.sharding import PartitionSpec as P

PANEL = 32


def from_root(value, axis, source):
    kept = jnp.where(lax.axis_index(axis) == source, value, 0).astype(value.dtype)
    return lax.psum(kept, axis)


def product(left, right):
    return jnp.dot(left, right, precision=lax.Precision.HIGHEST, preferred_element_type=jnp.float32)


def lower_half(matrix):
    return jnp.tril(matrix) - 0.5 * jnp.diag(jnp.diag(matrix))


def per_device(factor, adjoint, diag_inverse):
    rows_grid = lax.axis_size("row")
    cols_grid = lax.axis_size("col")
    my_row = lax.axis_index("row")
    my_col = lax.axis_index("col")
    row_blocks = adjoint.shape[0]
    width = adjoint.shape[2]
    col_blocks = adjoint.shape[3]
    lower = factor.reshape(row_blocks * width, col_blocks * width)
    grad = adjoint.reshape(row_blocks * width, col_blocks * width)
    global_rows = jnp.arange(row_blocks, dtype=jnp.int32) * rows_grid + my_row
    global_cols = jnp.arange(col_blocks, dtype=jnp.int32) * cols_grid + my_col
    for panel_step in range(2):
        block_index = PANEL - panel_step
        root_row = block_index % rows_grid
        root_col = block_index % cols_grid
        row_start = block_index // rows_grid * width
        col_start = block_index // cols_grid * width
        on_row = my_row == root_row
        on_col = my_col == root_col
        row_keep = jnp.repeat(global_rows > block_index, width)[:, None]
        col_keep = jnp.repeat(global_cols < block_index, width)[None, :]
        inverse = diag_inverse[panel_step]
        row_piece = from_root(lower[row_start : row_start + width, :], "row", root_row)
        row_factor = jnp.where(col_keep, row_piece, 0.0)
        left_factor = jnp.where(col_keep, lower, 0.0)
        grad_slab, factor_slab = (
            from_root(grad[:, col_start : col_start + width], "col", root_col),
            from_root(lower[:, col_start : col_start + width], "col", root_col),
        )
        below = product(jnp.where(row_keep, grad_slab, 0.0), inverse)
        diag_term = jnp.where(on_row, grad_slab[row_start : row_start + width], 0.0) - product(
            below.T, factor_slab
        )
        diag_factor = jnp.where(on_row, factor_slab[row_start : row_start + width], 0.0)
        cross_term = product(below.T, left_factor)
        diag_sum, factor_sum, cross_sum = lax.psum((diag_term, diag_factor, cross_term), "row")
        dbar = jnp.tril(diag_sum)
        inner = lower_half(product(jnp.tril(factor_sum).T, dbar))
        sym_part = product(product(inverse.T, inner), inverse)
        dbar = lower_half(sym_part + sym_part.T)
        grad = grad - product(below, row_factor)
        row_update = cross_sum + product(dbar + dbar.T, row_factor)
        new_rows = grad[row_start : row_start + width] - jnp.where(on_row, row_update, 0.0)
        grad = grad.at[row_start : row_start + width].set(new_rows)
        old_slab = grad[:, col_start : col_start + width]
        new_slab = jnp.where(on_col & row_keep, below, old_slab)
        grad = grad.at[:, col_start : col_start + width].set(new_slab)
        old_block = grad[row_start : row_start + width, col_start : col_start + width]
        grad = grad.at[row_start : row_start + width, col_start : col_start + width].set(
            jnp.where(on_row & on_col, dbar, old_block)
        )
    return grad.reshape(adjoint.shape)


def solution(mesh):
    placed = (P(None, "row", None, None, "col", None), P(None, "row", None, None, "col", None), P())
    return jax.shard_map(
        per_device,
        mesh=mesh,
        in_specs=placed,
        out_specs=P(None, "row", None, None, "col", None),
        check_vma=False,
    )
```

profile of v0, /device:TPU:1, one launch (start us, length us, event | category | flops | bytes accessed | tf_op | source)
XLA Modules:
  0.0 567.9 jit_solution(3878990912081606940)
XLA Ops:
  6.5 14.1 %reduce.24 = f32[4,256,4,256]{3,2,1,0:T(4,128)} reduce(f32[4,1,256,4,1,256]{5,4,3,2,1,0:T(1,128)} %param.15, f32[]{:T(128)} %constant.262), dimensions={1,4}, to_apply=%param.15.reduce_sub_computation | reduce | bytes 8388612 | tf_op args[0]
  20.6 5.1 copy.12
  25.8 14.1 %reduce.22 = f32[4,256,4,256]{3,2,1,0:T(4,128)} reduce(f32[4,1,256,4,1,256]{5,4,3,2,1,0:T(1,128)} %param.16, f32[]{:T(128)} %constant.262), dimensions={1,4}, to_apply=%param.16.reduce_sub_computation | reduce | bytes 8388612 | tf_op args[1]
  39.9 3.4 copy.10
  46.8 7.7 %fusion.15 = (f32[256,4,256]{2,1,0:T(4,128)S(1)}, f32[256,4,256]{2,1,0:T(4,128)S(1)}) fusion(pred[]{:T(512)S(6)} %eq.42, f32[4,1,256,4,1,256]{5,4,3,2,1,0:T(1,128)} %param.15, pred[]{:T(512)S(6)} %eq.38), kind=kLoop, calls=%fused_computation.29 | loop fusion | flops 524288 | bytes 4194306 | tf_op jit(solution)/shard_map/jit(_where)/select_n | solution.py:10
  55.7 109.3 %all-reduce.11.cloned.1.call-done = (f32[1024,256]{1,0:T(8,128)}, f32[1024,256]{1,0:T(8,128)}) async-done(((f32[1024,256]{1,0:T(8,128)}, f32[1024,256]{1,0:T(8,128)}), (f32[1024,256]{1,0:T(8,128)}, f32[1024,256]{1,0:T(8,128)})) %all-reduce.11.cloned.1.call-update) | async-done | bytes 2097168 | tf_op jit(solution)/shard_map/psum | solution.py:11
  166.8 2.2 fusion.18
  169.1 3.9 convolution_subtract_fusion.3
  173.0 4.7 fusion.2
  179.0 102.3 %all-reduce.15.cloned.1.call-done = (f32[256,1024]{1,0:T(8,128)}, f32[256,1024]{1,0:T(8,128)}, f32[256,256]{1,0:T(8,128)}, f32[256,256]{1,0:T(8,128)}) async-done(((f32[256,1024]{1,0:T(8,128)}, f32[256,1024]{1,0:T(8,128)}, f32[256,256]{1,0:T(8,128)}, f32[256,256]{1,0:T(8,128)}), (f32[256,1024]{1,0:T(8,128)}, f32[256,1024]{1,0:T(8,128)}, f32[256,256]{1,0:T(8,128)}, ...) | async-done | bytes 2621456 | tf_op jit(solution)/shard_map/psum | solution.py:11
  282.8 2.3 gather_fusion
  286.6 2.3 gather_fusion.1
  288.9 5.9 %convolution_subtract_fusion.1 = f32[1024,1024]{1,0:T(8,128)S(1)} fusion(f32[1024,1024]{1,0:T(8,128)} %bitcast.47, f32[1024,256]{1,0:T(8,128)S(1)} %fusion.18, f32[256,1024]{1,0:T(8,128)} %get-tuple-element.87, pred[1024]{0:T(1024)(128)(4,1)S(1)} %broadcast_in_dim.174), kind=kOutput, calls=%fused_computation.9 | convolution fusion | flops 3222536192 | bytes 10486784 | tf_op jit(solution)/shard_map/dot_general | solution.py:15
  302.0 113.2 %all-reduce.9.cloned.1.call-done = (f32[1024,256]{1,0:T(8,128)}, f32[1024,256]{1,0:T(8,128)}) async-done(((f32[1024,256]{1,0:T(8,128)}, f32[1024,256]{1,0:T(8,128)}), (f32[1024,256]{1,0:T(8,128)}, f32[1024,256]{1,0:T(8,128)})) %all-reduce.9.cloned.1.call-update) | async-done | bytes 2097168 | tf_op jit(solution)/shard_map/psum | solution.py:11
  417.1 2.3 fusion.16
  419.3 3.9 convolution_subtract_fusion.2
  423.2 4.7 fusion
  428.9 102.7 %all-reduce.13.cloned.1.call-done = (f32[256,1024]{1,0:T(8,128)}, f32[256,1024]{1,0:T(8,128)}, f32[256,256]{1,0:T(8,128)}, f32[256,256]{1,0:T(8,128)}) async-done(((f32[256,1024]{1,0:T(8,128)}, f32[256,1024]{1,0:T(8,128)}, f32[256,256]{1,0:T(8,128)}, f32[256,256]{1,0:T(8,128)}), (f32[256,1024]{1,0:T(8,128)}, f32[256,1024]{1,0:T(8,128)}, f32[256,256]{1,0:T(8,128)}, ...) | async-done | bytes 2621456 | tf_op jit(solution)/shard_map/psum | solution.py:11
  533.2 2.3 gather_fusion.2
  536.9 2.3 gather_fusion.3
  539.3 6.7 %convolution_subtract_fusion = f32[1024,1024]{1,0:T(8,128)} fusion(f32[1024,1024]{1,0:T(8,128)} %copy-done.3, f32[1024,256]{1,0:T(8,128)S(1)} %fusion.16, f32[256,1024]{1,0:T(8,128)S(1)} %copy-done.7, pred[1024]{0:T(1024)(128)(4,1)S(1)} %broadcast_in_dim.189), kind=kOutput, calls=%fused_computation.8 | convolution fusion | flops 3222536192 | bytes 10486784 | tf_op jit(solution)/shard_map/dot_general | solution.py:15
  546.0 3.4 fusion.10
  549.4 3.3 constant_dynamic-update-slice_fusion
  553.5 7.6 %reshape.218 = f32[4,1,256,4,1,256]{5,4,3,2,1,0:T(1,128)} reshape(f32[1024,1024]{1,0:T(8,128)} %fusion.36) | data formatting | bytes 8388608 | tf_op jit(solution)/shard_map/reshape | solution.py:74
  (65 shorter events, 24.3 us)
Async XLA Ops:
  6.5 158.5 %all-reduce.11.cloned.1.call-start = ((), (), s32[]{:S(2)}) async-start(), calls=%async_computation.1 | async-start | bytes 4194304 | tf_op jit(solution)/shard_map/psum | solution.py:11
  39.9 3.4 copy-start
  43.3 3.0 copy-start.4
  46.2 120.6 %copy-start.5 = (f32[2,256,256]{2,1,0:T(8,128)S(1)}, f32[2,256,256]{2,1,0:T(8,128)}, u32[]{:S(2)}) copy-start(f32[2,256,256]{2,1,0:T(8,128)} %param.17) | copy-start | bytes 1572868
  46.2 235.1 %all-reduce.15.cloned.1.call-start = ((), (), s32[]{:S(2)}) async-start(), calls=%async_computation.3 | async-start | bytes 5242880 | tf_op jit(solution)/shard_map/psum | solution.py:11
  165.0 8.0 %copy-start.1 = (f32[128,8,4,256]{3,1,2,0:T(8,128)S(1)}, f32[128,8,4,256]{3,1,2,0:T(8,128)}, u32[]{:S(2)}) copy-start(f32[128,8,4,256]{3,1,2,0:T(8,128)} %copy.12) | copy-start | bytes 12582916
  177.7 237.5 %all-reduce.9.cloned.1.call-start = ((), (), s32[]{:S(2)}) async-start(), calls=%async_computation | async-start | bytes 4194304 | tf_op jit(solution)/shard_map/psum | solution.py:11
  288.9 5.9 %copy-start.6 = (f32[256,1024]{1,0:T(8,128)S(1)}, f32[256,1024]{1,0:T(8,128)}, u32[]{:S(2)}) copy-start(f32[256,1024]{1,0:T(8,128)} %get-tuple-element.87) | copy-start | bytes 3145732
  288.9 5.9 %copy-start.8 = (f32[256,1024]{1,0:T(8,128)S(1)}, f32[256,1024]{1,0:T(8,128)}, u32[]{:S(2)}) copy-start(f32[256,1024]{1,0:T(8,128)} %get-tuple-element.88) | copy-start | bytes 3145732
  297.1 2.0 copy-start.3
  300.4 231.2 %all-reduce.13.cloned.1.call-start = ((), (), s32[]{:S(2)}) async-start(), calls=%async_computation.2 | async-start | bytes 5242880 | tf_op jit(solution)/shard_map/psum | solution.py:11
  415.2 8.0 %copy-start.2 = (f32[128,8,4,256]{3,1,2,0:T(8,128)S(1)}, f32[128,8,4,256]{3,1,2,0:T(8,128)}, u32[]{:S(2)}) copy-start(f32[128,8,4,256]{3,1,2,0:T(8,128)} %copy.12) | copy-start | bytes 12582916
  531.6 7.7 %copy-start.7 = (f32[256,1024]{1,0:T(8,128)S(1)}, f32[256,1024]{1,0:T(8,128)}, u32[]{:S(2)}) copy-start(f32[256,1024]{1,0:T(8,128)} %get-tuple-element.83) | copy-start | bytes 3145732
  539.2 6.7 %copy-start.9 = (f32[256,1024]{1,0:T(8,128)S(1)}, f32[256,1024]{1,0:T(8,128)}, u32[]{:S(2)}) copy-start(f32[256,1024]{1,0:T(8,128)} %get-tuple-element.84) | copy-start | bytes 3145732
Sparse Core Ops, SparseCore 0:
  46.4 118.6 all-reduce.10
  177.9 103.4 all-reduce.14
  300.5 114.6 all-reduce.8
  428.1 103.4 all-reduce.12
where the time goes:
time: 574 us; the launch traced here: 568 us
  waiting for transfers between devices  428 us (75%)
  other arithmetic  49.5 us (9%)
  matrix products  44.5 us (8%)
  local copies, waits for them, and re-layouts  31.5 us (5%)
  between operations  13.6 us (2%)
    psum x4, waiting for transfers between devices, from_root(): return lax.psum(kept, axis)  428 us
    dot_general x16, matrix products, product(): jnp.dot(left, right, precision=lax.Precision.HIGHEST, preferred_element_t...  44.5 us
    unnamed x2, other arithmetic  28.2 us
    unnamed x24, local copies, waits for them, and re-layouts  13.9 us
  transfers between devices with their start and end apart: 4, of which 4 were waited for; matrix products, arithmetic and copies ran while one was open for 2% of the time, Pallas kernels for 0%

commit v1 on v0

v1 whole, which is shorter than its diff:
```python
import functools

import jax
import jax.numpy as jnp
from jax import lax
from jax.experimental import pallas as pl
from jax.experimental.pallas import tpu as pltpu
from jax.sharding import PartitionSpec as P

W = 256
LANES = 128
SUB = 8
ROWS = W * SUB
F32 = jnp.float32
ANY = pl.BlockSpec(memory_space=pl.ANY)
VMEM = pl.BlockSpec(memory_space=pltpu.VMEM)
SMEM = pl.BlockSpec(memory_space=pltpu.SMEM)


def product(left, right):
    return jnp.dot(left, right, precision=lax.Precision.HIGHEST, preferred_element_type=F32)


def product_t(left, right):
    return lax.dot_general(
        left, right, (((0,), (0,)), ((), ())), precision=lax.Precision.HIGHEST, preferred_element_type=F32
    )


def product_nt(left, right):
    return lax.dot_general(
        left, right, (((1,), (1,)), ((), ())), precision=lax.Precision.HIGHEST, preferred_element_type=F32
    )


def masks(size):
    rows = lax.broadcasted_iota(jnp.int32, (size, size), 0)
    cols = lax.broadcasted_iota(jnp.int32, (size, size), 1)
    return rows >= cols, rows == cols


def tril(matrix):
    return jnp.where(masks(matrix.shape[0])[0], matrix, 0.0)


def lower_half(matrix):
    low, diag = masks(matrix.shape[0])
    return jnp.where(diag, 0.5 * matrix, jnp.where(low, matrix, 0.0))


def call(body, out_shape, in_specs, out_specs, scratch, flops, moved, alias=None):
    return pl.pallas_call(
        body,
        out_shape=out_shape,
        in_specs=in_specs,
        out_specs=out_specs,
        scratch_shapes=scratch,
        input_output_aliases=alias or {},
        compiler_params=pltpu.CompilerParams(vmem_limit_bytes=60 * 1024 * 1024),
        cost_estimate=pl.CostEstimate(flops=flops, bytes_accessed=moved, transcendentals=0),
    )


def shape(*dims):
    return jax.ShapeDtypeStruct(dims, F32)


def piece_of(buf, first, rows, k):
    return buf[pl.ds(first * SUB + k, rows, stride=SUB), :]


def entry_kernel(pos, g, l, slab, piece, gbuf, lbuf, sems):
    odd_row = pos[0] % 2
    odd_col = pos[1] % 2
    first = pltpu.make_async_copy(g.at[pl.ds(2 * ROWS, 2 * ROWS)], gbuf, sems.at[0])
    first.start()
    start = pl.multiple_of((2 - odd_row) * ROWS, ROWS)
    second = pltpu.make_async_copy(l.at[pl.ds(start, ROWS)], lbuf, sems.at[1])
    second.start()
    first.wait()
    for odd in range(2):

        @pl.when(odd_col == odd)
        def _():
            for h in range(2):
                slab[:, h * LANES : (h + 1) * LANES] = piece_of(gbuf, 0, 2 * W, 2 * (2 - odd) + h)

    second.wait()
    for k in range(4):
        piece[:, k * LANES : (k + 1) * LANES] = piece_of(lbuf, 0, W, k)


def unpack_kernel(pos, g, l, inside, fslab, corner, ldiag, lbuf, gbuf, sems):
    odd_col = pos[1] % 2
    first = pltpu.make_async_copy(l.at[pl.ds(2 * ROWS, 2 * ROWS)], lbuf, sems.at[0])
    first.start()
    second = pltpu.make_async_copy(g.at[pl.ds(ROWS, ROWS)], gbuf, sems.at[1])
    second.start()
    first.wait()
    for odd in range(2):

        @pl.when(odd_col == odd)
        def _():
            for h in range(2):
                fslab[:, h * LANES : (h + 1) * LANES] = piece_of(lbuf, 0, 2 * W, 2 * (2 - odd) + h)

    for k in range(4):
        inside[:, k * LANES : (k + 1) * LANES] = piece_of(lbuf, 0, 2 * W, k)
    for h in range(2):
        ldiag[:, h * LANES : (h + 1) * LANES] = piece_of(lbuf, 0, W, 4 + h)
    second.wait()
    for h in range(2):
        corner[:, h * LANES : (h + 1) * LANES] = piece_of(gbuf, 0, W, 2 + h)


def pick(pos, axis, mine, other):
    odd = pos[axis] % 2 == 1
    return jnp.where(odd, other, mine), jnp.where(odd, mine, other)


def live_rows(pos, value):
    rows = lax.broadcasted_iota(jnp.int32, value.shape, 0)
    return jnp.where((pos[0] == 0) & (rows < W), 0.0, value)


def diag_kernel(pos, sent, slab, fslab, out):
    right = fslab[...]
    left = jnp.where(pos[1] % 2 == 1, sent[...], slab[...])
    out[:W] = product_t(live_rows(pos, left), right)
    out[W:] = product_t(live_rows(pos, slab[...]), right)


def sums_kernel(pos, mine, other, inside, out):
    g32, g31 = pick(pos, 1, mine[...], other[...])
    right = inside[...]
    out[:W] = product_t(live_rows(pos, g32), right)
    out[W:] = product_t(live_rows(pos, g31), right)


def bulk_kernel(pos, g, gmine, gother, rmine, rother, smine, sother, z, out, gbuf, abuf, b0, b1, sems):
    load = pltpu.make_async_copy(g.at[pl.ds(2 * ROWS, 2 * ROWS)], gbuf, sems.at[0])
    load.start()
    above = pltpu.make_async_copy(g.at[pl.ds(0, 2 * ROWS)], abuf, sems.at[1])
    above.start()
    g32, g31 = pick(pos, 1, gmine[...], gother[...])
    row32, row31 = pick(pos, 0, rmine[...], rother[...])
    l3231 = jnp.where(pos[1] % 2 == 1, smine[:W], sother[:W])
    below0 = product(g32, z[0])
    b0[...] = below0
    below1 = product(g31 - product(below0, l3231), z[1])
    b1[...] = below1
    change = product(below0, row32) + product(below1, row31)
    above.wait()
    rest = pltpu.make_async_copy(abuf, out.at[pl.ds(0, 2 * ROWS)], sems.at[1])
    rest.start()
    load.wait()
    for k in range(4):
        at = pl.ds(k, 2 * W, stride=SUB)
        gbuf[at, :] = gbuf[at, :] - change[:, k * LANES : (k + 1) * LANES]

    @pl.when(pos[1] == 15)
    def _():
        for h in range(2):
            gbuf[pl.ds(2 + h, 2 * W, stride=SUB), :] = b1[:, h * LANES : (h + 1) * LANES]

    @pl.when(pos[1] == 0)
    def _():
        for h in range(2):
            gbuf[pl.ds(4 + h, 2 * W, stride=SUB), :] = b0[:, h * LANES : (h + 1) * LANES]

    store = pltpu.make_async_copy(gbuf, out.at[pl.ds(2 * ROWS, 2 * ROWS)], sems.at[0])
    store.start()
    rest.wait()
    store.wait()


def chain_one_kernel(pos, sums, gmine, gother, smine, sother, z, sym0, below_row):
    @pl.when(pos[0] == 0)
    def _():
        z0, z1 = z[0], z[1]
        g3232, g3231 = pick(pos, 1, gmine[:W], gother[:W])
        small0, small1 = pick(pos, 1, smine[:W], sother[:W])
        t32 = product_t(z0, sums[:W, :W])
        t31 = product_t(z0, sums[:W, W:])
        inner = lower_half(product_t(tril(small0), tril(g3232 - t32)))
        sym = product(product_t(z0, inner), z0)
        sym = sym + sym.T
        sym0[...] = sym
        below_row[...] = product(g3231 - t31 - product(sym, small1), z1)

    @pl.when(pos[0] != 0)
    def _():
        sym0[...] = jnp.zeros_like(sym0)
        below_row[...] = jnp.zeros_like(below_row)


def chain_two_kernel(pos, sums, smine, sother, below_row, z, sym1, mix):
    @pl.when(pos[0] == 15)
    def _():
        z0, z1 = z[0], z[1]
        small0, small1 = pick(pos, 1, smine[...], sother[...])
        l3231, l3131, g3131 = small1[:W], small1[W:], small0[W:]
        t31 = product_t(z0, sums[:W, W:])
        t31b = product_t(z1, sums[W:, W:] - product_t(l3231, t31))
        dbar = tril(g3131 - t31b - product_t(below_row[...], l3231))
        inner = lower_half(product_t(tril(l3131), dbar))
        sym = product(product_t(z1, inner), z1)
        sym1[...] = sym + sym.T
        mix[...] = product(z0, product(l3231, z1))

    @pl.when(pos[0] != 15)
    def _():
        sym1[...] = jnp.zeros_like(sym1)
        mix[...] = jnp.zeros_like(mix)


def finish_kernel(pos, g, sums, rmine, rother, sym0, b_here, b_sent, sym1, mix, z, done, out, gbuf, sem):
    def panel_row(first, update, corner, extra):
        load = pltpu.make_async_copy(g.at[pl.ds(first * ROWS, ROWS)], gbuf, sem)
        load.start()
        change = update()
        load.wait()
        for k in range(4):
            at = pl.ds(k, W, stride=SUB)
            gbuf[at, :] = gbuf[at, :] - change[:, k * LANES : (k + 1) * LANES]

        @pl.when(pos[1] == 15)
        def _():
            for h in range(2):
                gbuf[pl.ds(2 + h, W, stride=SUB), :] = corner()[:, h * LANES : (h + 1) * LANES]

        if extra is not None:

            @pl.when(pos[1] == 0)
            def _():
                for h in range(2):
                    gbuf[pl.ds(4 + h, W, stride=SUB), :] = extra()[:, h * LANES : (h + 1) * LANES]

        store = pltpu.make_async_copy(gbuf, out.at[pl.ds(first * ROWS, ROWS)], sem)
        store.start()
        store.wait()

    @pl.when(pos[0] == 0)
    def _():
        def update():
            row32, row31 = pick(pos, 0, rmine[...], rother[...])
            return (
                product_t(z[0], sums[:W]) + product(sym0[...], row32) + product(b_here[...], row31)
            )

        panel_row(2, update, lambda: b_here[...], lambda: lower_half(sym0[...]))

    @pl.when(pos[0] == 15)
    def _():
        def update():
            row32, row31 = pick(pos, 0, rmine[...], rother[...])
            return (
                product_t(z[1], sums[W:])
                - product_t(mix[...], sums[:W])
                + product_t(b_sent[...], row32)
                + product(sym1[...], row31)
            )

        panel_row(1, update, lambda: lower_half(sym1[...]), None)


def tree_step(value, axis, step):
    size = lax.axis_size(axis)
    reach = size >> (step + 1)
    pairs = [(h, h + reach) for h in range(0, size, 2 * reach)]
    pairs = pairs + [(size - 1 - s, size - 1 - t) for s, t in pairs]
    moved = lax.ppermute(value, axis, pairs)
    index = lax.axis_index(axis)
    got = functools.reduce(jnp.logical_or, [index == t for _, t in pairs])
    return jnp.where(got, moved, value)


def tree(value, axis):
    for step in range(3):
        value = tree_step(value, axis, step)
    return value


def after(value, *others):
    return lax.optimization_barrier((value, *others))[0]


def swap(value, axis):
    size = lax.axis_size(axis)
    return lax.ppermute(value, axis, [(i, i ^ 1) for i in range(size)])


def exchange(value, axis):
    size = lax.axis_size(axis)
    parts = value.reshape(size, value.shape[0] // size, value.shape[1])
    return lax.all_to_all(parts, axis, 0, 0)


def gather_parts(part, axis):
    size = lax.axis_size(axis)
    parts = jnp.broadcast_to(part[None], (size,) + part.shape)
    parts = lax.all_to_all(parts, axis, 0, 0)
    return parts.reshape(size * part.shape[0], part.shape[1])


def per_device(factor, adjoint, diag_inverse):
    my_row = lax.axis_index("row")
    my_col = lax.axis_index("col")
    pos = jnp.stack([my_row, my_col]).astype(jnp.int32)
    odd_col = my_col % 2 == 1
    g = adjoint.reshape(4 * ROWS, LANES)
    l = factor.reshape(4 * ROWS, LANES)
    z = diag_inverse
    dma = pltpu.SemaphoreType.DMA
    block = W * W * 4

    slab, piece = call(
        entry_kernel,
        (shape(2 * W, W), shape(W, 2 * W)),
        [SMEM, ANY, ANY],
        (VMEM, VMEM),
        [pltpu.VMEM((2 * ROWS, LANES), F32), pltpu.VMEM((ROWS, LANES), F32), dma((2,))],
        0,
        16 * block,
    )(pos, g, l)
    sent = lax.ppermute(slab, "col", [(0, 15)])
    gmine = tree_step(slab, "col", 0)
    rmine = tree_step(piece, "row", 0)
    gmine, rmine = after(gmine, rmine), after(rmine, gmine)
    inside, fslab, corner, ldiag = call(
        unpack_kernel,
        (shape(2 * W, 2 * W), shape(2 * W, W), shape(W, W), shape(W, W)),
        [SMEM, ANY, ANY],
        (VMEM,) * 4,
        [pltpu.VMEM((2 * ROWS, LANES), F32), pltpu.VMEM((ROWS, LANES), F32), dma((2,))],
        0,
        20 * block,
    )(pos, g, l)

    gmine2 = tree_step(gmine, "col", 1)
    rmine2 = tree_step(rmine, "row", 1)

    partial = call(
        diag_kernel, shape(2 * W, W), [SMEM] + [VMEM] * 3, VMEM, [], 8 * W**3, 8 * block
    )(pos, sent, slab, fslab)
    diag_parts = exchange(after(partial, gmine2, rmine2), "row")
    gmine, rmine = after(gmine2, rmine2, partial), after(rmine2, gmine2, partial)
    gmine, rmine = tree_step(gmine, "col", 2), tree_step(rmine, "row", 2)
    gmine, rmine = after(gmine, rmine), after(rmine, gmine)
    gother, rother = swap(gmine, "col"), swap(rmine, "row")
    diag_mine = tree(after(diag_parts, gother).sum(0), "col")
    diag_other = swap(diag_mine, "col")
    diag_cols = jnp.where(
        odd_col,
        jnp.concatenate([diag_other, diag_mine], axis=1),
        jnp.concatenate([diag_mine, diag_other], axis=1),
    )
    diag_sums = gather_parts(diag_cols, "row")

    sums = call(
        sums_kernel, shape(2 * W, 2 * W), [SMEM] + [VMEM] * 3, VMEM, [], 16 * W**3, 12 * block
    )(pos, gmine, gother, inside)
    sums = gather_parts(exchange(sums, "row").sum(0), "row")

    corner = lax.ppermute(corner, "col", [(15, 0)])
    at_first = jnp.concatenate([ldiag, corner], axis=0)
    odd_row = my_row % 2 == 1
    row32 = jnp.where(odd_row, rother[:, W:], rmine[:, W:])
    row31 = jnp.where(odd_row, rmine[:, W:], rother[:, W:])
    at_last = jnp.concatenate([row32, row31], axis=0)
    smine = tree(jnp.where(odd_col, at_last, at_first), "col")
    sother = swap(smine, "col")

    out = call(
        bulk_kernel,
        shape(4 * ROWS, LANES),
        [SMEM, ANY] + [VMEM] * 7,
        ANY,
        [
            pltpu.VMEM((2 * ROWS, LANES), F32),
            pltpu.VMEM((2 * ROWS, LANES), F32),
            pltpu.VMEM((2 * W, W), F32),
            pltpu.VMEM((2 * W, W), F32),
            dma((2,)),
        ],
        30 * W**3,
        40 * block,
    )(pos, g, gmine, gother, rmine, rother, smine, sother, z)

    sym0, below_row = call(
        chain_one_kernel, (shape(W, W),) * 2, [SMEM] + [VMEM] * 6, (VMEM,) * 2, [], 16 * W**3, 12 * block
    )(pos, diag_sums, gmine, gother, smine, sother, z)
    below_sent = lax.ppermute(below_row, "row", [(0, 15)])
    sym1, mix = call(
        chain_two_kernel, (shape(W, W),) * 2, [SMEM] + [VMEM] * 5, (VMEM,) * 2, [], 16 * W**3, 12 * block
    )(pos, diag_sums, smine, sother, below_sent, z)
    out = call(
        finish_kernel,
        shape(4 * ROWS, LANES),
        [SMEM, ANY] + [VMEM] * 9 + [ANY],
        ANY,
        [pltpu.VMEM((ROWS, LANES), F32), dma],
        16 * W**3,
        16 * block,
        alias={11: 0},
    )(pos, g, sums, rmine, rother, sym0, below_row, below_sent, sym1, mix, z, out)
    return out.reshape(adjoint.shape)


def solution(mesh):
    placed = (P(None, "row", None, None, "col", None), P(None, "row", None, None, "col", None), P())
    return jax.shard_map(
        per_device,
        mesh=mesh,
        in_specs=placed,
        out_specs=P(None, "row", None, None, "col", None),
        check_vma=False,
    )
```

time: 574 us -> 166 us (0.29)
  waiting for transfers between devices: 428 us -> 55.4 us
  starting transfers between devices: 1.12 us -> 59 us
  matrix products: 44.5 us -> 0 us
  other arithmetic: 49.5 us -> 5.79 us
  Pallas kernels: 0 us -> 36.5 us
  local copies, waits for them, and re-layouts: 31.5 us -> 5.66 us
  between operations: 13.6 us -> 0.69 us
    psum x4 -> x0, waiting for transfers between devices: 428 us -> none  [from_root(): return lax.psum(kept, axis)]
    dot_general x16 -> x0, matrix products: 44.5 us -> none  [product(): jnp.dot(left, right, precision=lax.Precision.HIGHEST, preferred_element_t...]
    ppermute x0 -> x19, starting transfers between devices: none -> 40.4 us  [the longest x12 17.7 us: tree_step(): moved = lax.ppermute(value, axis, pairs)]
    pallas_call x0 -> x8, Pallas kernels: none -> 36.5 us  [the longest x1 7.9 us: per_device(): call(bulk_kernel, shape(4 * ROWS, LANES), [SMEM, ANY] + [VMEM] * 7, ANY,...]
    ppermute x0 -> x19, waiting for transfers between devices: none -> 34.2 us  [the longest x12 31.8 us: tree_step(): moved = lax.ppermute(value, axis, pairs)]
    unnamed x2 -> x0, other arithmetic: 28.2 us -> none
    all_to_all x0 -> x4, waiting for transfers between devices: none -> 21.1 us  [the longest x2 14.2 us: gather_parts(): parts = lax.all_to_all(parts, axis, 0, 0)]
    all_to_all x0 -> x4, starting transfers between devices: none -> 18.6 us  [the longest x2 11.4 us: gather_parts(): parts = lax.all_to_all(parts, axis, 0, 0)]
  transfers between devices with their start and end apart: 4 -> 23, of which waited for: 4 -> 7; matrix products, arithmetic and copies ran while one was open for 2% -> 4% of each run, Pallas kernels for 0% -> 17%
where the time goes in v1:
time: 166 us; the launch traced here: 163 us
  starting transfers between devices  59 us (36%)
  waiting for transfers between devices  55.4 us (33%)
  Pallas kernels  36.5 us (22%)
  other arithmetic  5.79 us (3%)
  local copies, waits for them, and re-layouts  5.66 us (3%)
    ppermute x12, waiting for transfers between devices, tree_step(): moved = lax.ppermute(value, axis, pairs)  31.8 us
    ppermute x12, starting transfers between devices, tree_step(): moved = lax.ppermute(value, axis, pairs)  17.7 us
    ppermute x4, starting transfers between devices, swap(): return lax.ppermute(value, axis, [(i, i ^ 1) for i in range(size)])  16.8 us
    all_to_all x2, waiting for transfers between devices, gather_parts(): parts = lax.all_to_all(parts, axis, 0, 0)  14.2 us
    all_to_all x2, starting transfers between devices, gather_parts(): parts = lax.all_to_all(parts, axis, 0, 0)  11.4 us
    pallas_call x1, Pallas kernels, per_device(): call(bulk_kernel, shape(4 * ROWS, LANES), [SMEM, ANY] + [VMEM] * 7, ANY,...  7.9 us
    all_to_all x2, starting transfers between devices, exchange(): return lax.all_to_all(parts, axis, 0, 0)  7.23 us
    all_to_all x2, waiting for transfers between devices, exchange(): return lax.all_to_all(parts, axis, 0, 0)  6.94 us
  transfers between devices with their start and end apart: 23, of which 7 were waited for; matrix products, arithmetic and copies ran while one was open for 4% of the time, Pallas kernels for 17%

profile of v1, /device:TPU:1, one launch (start us, length us, event | category | flops | bytes accessed | tf_op | source)
XLA Modules:
  0.0 163.0 jit_solution(5915149184808672808)
XLA Ops:
  0.6 3.5 %shard_map.37 = (f32[512,256]{1,0:T(8,128)}, f32[256,512]{1,0:T(8,128)}) custom-call(s32[2]{0:T(128)} %pad_add_fusion.pos, f32[8192,128]{1,0:T(8,128)} %bitcast.9, f32[8192,128]{1,0:T(8,128)} %bitcast.13), custom_call_target="tpu_custom_call" | custom-call | bytes 4194304 | tf_op jit(solution)/shard_map/pallas_call | solution.py:317
  4.2 5.5 %collective-permute-start.1 = (f32[256,512]{1,0:T(8,128)}, f32[256,512]{1,0:T(8,128)S(1)}, u32[]{:S(2)}, u32[]{:S(2)}) collective-permute-start(f32[256,512]{1,0:T(8,128)} %get-tuple-element.24), channel_id=1, source_target_pairs={{0,128},{240,112},{1,129},{241,113},{2,130},{242,114},{3,131},{243... | collective-permute-start | bytes 1572872 | tf_op jit(solution)/shard_map/ppermute | solution.py:272
  11.1 9.4 %collective-permute-done.1 = f32[256,512]{1,0:T(8,128)S(1)} collective-permute-done((f32[256,512]{1,0:T(8,128)}, f32[256,512]{1,0:T(8,128)S(1)}, u32[]{:S(2)}, u32[]{:S(2)}) %collective-permute-start.1) | collective-permute-done | bytes 524320 | tf_op jit(solution)/shard_map/ppermute | solution.py:272
  24.9 4.0 %shard_map.38 = (f32[512,512]{1,0:T(8,128)}, f32[512,256]{1,0:T(8,128)}, f32[256,256]{1,0:T(8,128)}, f32[256,256]{1,0:T(8,128)}) custom-call(s32[2]{0:T(128)} %pad_add_fusion.pos, f32[8192,128]{1,0:T(8,128)} %bitcast.10, f32[8192,128]{1,0:T(8,128)} %bitcast.14), custom_call_target="tpu_custom_call" | custom-call | bytes 5242880 | tf_op jit(solution)/shard_map/pallas_call | solution.py:330
  29.7 3.3 %shard_map.39 = f32[512,256]{1,0:T(8,128)} custom-call(s32[2]{0:T(128)} %pad_add_fusion.pos, f32[512,256]{1,0:T(8,128)} %copy-done.9, f32[512,256]{1,0:T(8,128)} %get-tuple-element.23.slab, f32[512,256]{1,0:T(8,128)} %get-tuple-element.27.fslab), custom_call_target="tpu_custom_call" | custom-call | flops 134217728 | bytes 2097152 | tf_op jit(solution)/shard_map/pallas_call | solution.py:343
  35.9 9.7 %collective-permute-done.5 = f32[512,256]{1,0:T(8,128)S(1)} collective-permute-done((f32[512,256]{1,0:T(8,128)S(1)}, f32[512,256]{1,0:T(8,128)S(1)}, u32[]{:S(2)}, u32[]{:S(2)}) %collective-permute-start.5) | collective-permute-done | bytes 524320 | tf_op jit(solution)/shard_map/ppermute | solution.py:272
  45.9 12.5 %collective-permute-start.7 = (f32[512,256]{1,0:T(8,128)S(1)}, f32[512,256]{1,0:T(8,128)S(1)}, u32[]{:S(2)}, u32[]{:S(2)}) collective-permute-start(f32[512,256]{1,0:T(8,128)S(1)} %broadcast_select_fusion.8.mine.gmine), channel_id=1, source_target_pairs={{0,1},{1,0},{2,3},{3,2},{4,5},{5,4},{6,7},{7,6},{8,9},{9,8},{10,11... | collective-permute-start | bytes 1572872 | tf_op jit(solution)/shard_map/ppermute | solution.py:290
  58.3 3.6 %all-to-all-start.2 = ((f32[16,32,256]{2,1,0:T(8,128)}), f32[16,32,256]{2,1,0:T(8,128)S(1)}, u32[]{:S(2)}, u32[]{:S(2)}) async-start(f32[16,32,256]{2,1,0:T(8,128)} %bitcast.6), calls=%async_computation.2 | async-start | bytes 1048576 | tf_op jit(solution)/shard_map/all_to_all | solution.py:296
  64.5 1.5 collective-permute-start.14
  66.0 6.9 %all-to-all-done.2 = f32[16,32,256]{2,1,0:T(8,128)S(1)} async-done(((f32[16,32,256]{2,1,0:T(8,128)}), f32[16,32,256]{2,1,0:T(8,128)S(1)}, u32[]{:S(2)}, u32[]{:S(2)}) %all-to-all-start.2) | async-done | bytes 524320 | tf_op jit(solution)/shard_map/all_to_all | solution.py:296
  73.7 4.5 %shard_map.40 = f32[512,512]{1,0:T(8,128)} custom-call(s32[2]{0:T(128)} %pad_add_fusion.pos, f32[512,256]{1,0:T(8,128)} %copy-done.1, f32[512,256]{1,0:T(8,128)} %copy-done.4, f32[512,512]{1,0:T(8,128)} %get-tuple-element.31.inside), custom_call_target="tpu_custom_call" | custom-call | flops 268435456 | bytes 3145728 | tf_op jit(solution)/shard_map/pallas_call | solution.py:360
  78.2 3.7 %all-to-all-start = ((f32[16,32,512]{2,1,0:T(8,128)}), f32[16,32,512]{2,1,0:T(8,128)S(1)}, u32[]{:S(2)}, u32[]{:S(2)}) async-start(f32[16,32,512]{2,1,0:T(8,128)} %bitcast.18), calls=%async_computation | async-start | bytes 2097152 | tf_op jit(solution)/shard_map/all_to_all | solution.py:296
  84.0 1.5 collective-permute-start.15
  85.4 12.7 %collective-permute-done.11 = f32[32,256]{1,0:T(8,128)S(1)} collective-permute-done((f32[32,256]{1,0:T(8,128)S(1)}, f32[32,256]{1,0:T(8,128)S(1)}, u32[]{:S(2)}, u32[]{:S(2)}) %collective-permute-start.11) | collective-permute-done | bytes 32800 | tf_op jit(solution)/shard_map/ppermute | solution.py:272
  98.1 2.9 %collective-permute-start.12 = (f32[32,256]{1,0:T(8,128)S(1)}, f32[32,256]{1,0:T(8,128)S(1)}, u32[]{:S(2)}, u32[]{:S(2)}) collective-permute-start(f32[32,256]{1,0:T(8,128)S(1)} %broadcast_select_fusion.11), channel_id=1, source_target_pairs={{0,1},{1,0},{2,3},{3,2},{4,5},{5,4},{6,7},{7,6},{8,9},{9,8},{10,11... | collective-permute-start | bytes 98312 | tf_op jit(solution)/shard_map/ppermute | solution.py:290
  103.0 6.9 %all-to-all-start.3 = ((f32[16,32,512]{2,1,0:T(8,128)}), f32[16,32,512]{2,1,0:T(8,128)S(1)}, u32[]{:S(2)}, u32[]{:S(2)}) async-start(f32[16,32,512]{2,1,0:T(8,128)} %broadcast_in_dim.5), calls=%async_computation.3 | async-start | bytes 2097152 | tf_op jit(solution)/shard_map/all_to_all | solution.py:302
  111.4 14.2 %all-to-all-done.3 = f32[16,32,512]{2,1,0:T(8,128)S(1)} async-done(((f32[16,32,512]{2,1,0:T(8,128)}), f32[16,32,512]{2,1,0:T(8,128)S(1)}, u32[]{:S(2)}, u32[]{:S(2)}) %all-to-all-start.3) | async-done | bytes 1048608 | tf_op jit(solution)/shard_map/all_to_all | solution.py:302
  126.8 4.5 %all-to-all-start.1 = ((f32[16,32,512]{2,1,0:T(8,128)}), f32[16,32,512]{2,1,0:T(8,128)S(1)}, u32[]{:S(2)}, u32[]{:S(2)}) async-start(f32[16,32,512]{2,1,0:T(8,128)} %broadcast_in_dim.4), calls=%async_computation.1 | async-start | bytes 2097152 | tf_op jit(solution)/shard_map/all_to_all | solution.py:302
  133.7 1.5 collective-permute-done.17.sother
  136.1 5.9 %shard_map.41 = (f32[256,256]{1,0:T(8,128)}, f32[256,256]{1,0:T(8,128)}) custom-call(s32[2]{0:T(128)} %pad_add_fusion.pos, f32[512,512]{1,0:T(8,128)} %bitcast.15, f32[512,256]{1,0:T(8,128)} %copy-done.1, f32[512,256]{1,0:T(8,128)} %copy-done.4, f32[512,256]{1,0:T(8,128)} %copy-done.2, f32[512,256]{1,0:T(8,128)} %copy-done.5, f32[2,256,256]{2,1,0:T(8,128)} %z.7), custom_call_target="tpu_custom_call" | custom-call | flops 268435456 | bytes 3145728 | tf_op jit(solution)/shard_map/pallas_call | solution.py:390
  142.0 3.9 %collective-permute-start.18 = (f32[256,256]{1,0:T(8,128)}, f32[256,256]{1,0:T(8,128)S(1)}, u32[]{:S(2)}, u32[]{:S(2)}) collective-permute-start(f32[256,256]{1,0:T(8,128)} %get-tuple-element.38.b_here), channel_id=1, source_target_pairs={{0,240},{1,241},{2,242},{3,243},{4,244},{5,245},{6,246},{7,247},{8... | collective-permute-start | bytes 786440 | tf_op jit(solution)/shard_map/ppermute | solution.py:393
  145.9 7.9 %shard_map.43.done = f32[8192,128]{1,0:T(8,128)} custom-call(s32[2]{0:T(128)} %pad_add_fusion.pos, f32[8192,128]{1,0:T(8,128)} %bitcast.11, f32[512,256]{1,0:T(8,128)} %copy-done.1, f32[512,256]{1,0:T(8,128)} %copy-done.4, f32[256,512]{1,0:T(8,128)} %copy-done.3, f32[256,512]{1,0:T(8,128)} %copy-done.7, f32[512,256]{1,0:T(8,128)} %copy-done.2, ...), custom_call_target="tpu_custom_call" | custom-call | flops 503316480 | bytes 10485760 | tf_op jit(solution)/shard_map/pallas_call | solution.py:374
  154.6 2.6 %shard_map.42 = (f32[256,256]{1,0:T(8,128)}, f32[256,256]{1,0:T(8,128)}) custom-call(s32[2]{0:T(128)} %pad_add_fusion.pos, f32[512,512]{1,0:T(8,128)} %bitcast.16, f32[512,256]{1,0:T(8,128)} %copy-done.2, f32[512,256]{1,0:T(8,128)} %copy-done.5, f32[256,256]{1,0:T(8,128)} %copy-done.8, f32[2,256,256]{2,1,0:T(8,128)} %z.7), custom_call_target="tpu_custom_call" | custom-call | flops 268435456 | bytes 3145728 | tf_op jit(solution)/shard_map/pallas_call | solution.py:394
  158.1 4.7 %shard_map.44 = f32[8192,128]{1,0:T(8,128)} custom-call(s32[2]{0:T(128)} %pad_add_fusion.pos, f32[8192,128]{1,0:T(8,128)} %bitcast.12, f32[512,512]{1,0:T(8,128)} %bitcast.17, f32[256,512]{1,0:T(8,128)} %copy-done.3, f32[256,512]{1,0:T(8,128)} %copy-done.7, f32[256,256]{1,0:T(8,128)} %get-tuple-element.37.sym0, ...), custom_call_target="tpu_custom_call", output_to_operand_aliasing={{}: (11, {})} | custom-call | flops 268435456 | bytes 4194304 | tf_op jit(solution)/shard_map/pallas_call | solution.py:397
  (72 shorter events, 25.0 us)
Async XLA Ops:
  4.2 16.4 %collective-permute-start.1 = (f32[256,512]{1,0:T(8,128)}, f32[256,512]{1,0:T(8,128)S(1)}, u32[]{:S(2)}, u32[]{:S(2)}) collective-permute-start(f32[256,512]{1,0:T(8,128)} %get-tuple-element.24), channel_id=1, source_target_pairs={{0,128},{240,112},{1,129},{241,113},{2,130},{242,114},{3,131},{243... | collective-permute-start | bytes 1572872 | tf_op jit(solution)/shard_map/ppermute | solution.py:272
  9.7 12.0 %collective-permute-start = (f32[512,256]{1,0:T(8,128)}, f32[512,256]{1,0:T(8,128)S(1)}, u32[]{:S(2)}, u32[]{:S(2)}) collective-permute-start(f32[512,256]{1,0:T(8,128)} %get-tuple-element.23.slab), channel_id=1, source_target_pairs={{0,8},{15,7},{16,24},{31,23},{32,40},{47,39},{48,56},{63,55},{64,7... | collective-permute-start | bytes 1572872 | tf_op jit(solution)/shard_map/ppermute | solution.py:272
  10.4 18.5 %collective-permute-start.4 = (f32[512,256]{1,0:T(8,128)}, f32[512,256]{1,0:T(8,128)S(1)}, u32[]{:S(2)}, u32[]{:S(2)}) collective-permute-start(f32[512,256]{1,0:T(8,128)} %get-tuple-element.23.slab), channel_id=1, source_target_pairs={{0,15},{16,31},{32,47},{48,63},{64,79},{80,95},{96,111},{112,127},... | collective-permute-start | bytes 1572872 | tf_op jit(solution)/shard_map/ppermute | solution.py:326
  22.8 10.2 %collective-permute-start.2 = (f32[512,256]{1,0:T(8,128)S(1)}, f32[512,256]{1,0:T(8,128)S(1)}, u32[]{:S(2)}, u32[]{:S(2)}) collective-permute-start(f32[512,256]{1,0:T(8,128)S(1)} %broadcast_select_fusion.4), channel_id=1, source_target_pairs={{0,4},{8,12},{15,11},{7,3},{16,20},{24,28},{31,27},{23,19},{32,36}... | collective-permute-start | bytes 1572872 | tf_op jit(solution)/shard_map/ppermute | solution.py:272
  23.5 9.6 %collective-permute-start.3 = (f32[256,512]{1,0:T(8,128)S(1)}, f32[256,512]{1,0:T(8,128)S(1)}, u32[]{:S(2)}, u32[]{:S(2)}) collective-permute-start(f32[256,512]{1,0:T(8,128)S(1)} %broadcast_select_fusion.2), channel_id=1, source_target_pairs={{0,64},{128,192},{240,176},{112,48},{1,65},{129,193},{241,177},{11... | collective-permute-start | bytes 1572872 | tf_op jit(solution)/shard_map/ppermute | solution.py:272
  33.2 12.4 %collective-permute-start.5 = (f32[512,256]{1,0:T(8,128)S(1)}, f32[512,256]{1,0:T(8,128)S(1)}, u32[]{:S(2)}, u32[]{:S(2)}) collective-permute-start(f32[512,256]{1,0:T(8,128)S(1)} %broadcast_select_fusion.6), channel_id=1, source_target_pairs={{0,2},{4,6},{8,10},{12,14},{15,13},{11,9},{7,5},{3,1},{16,18},{20,... | collective-permute-start | bytes 1572872 | tf_op jit(solution)/shard_map/ppermute | solution.py:272
  34.5 11.1 %collective-permute-start.6 = (f32[256,512]{1,0:T(8,128)S(1)}, f32[256,512]{1,0:T(8,128)S(1)}, u32[]{:S(2)}, u32[]{:S(2)}) collective-permute-start(f32[256,512]{1,0:T(8,128)S(1)} %broadcast_select_fusion.1), channel_id=1, source_target_pairs={{0,32},{64,96},{128,160},{192,224},{240,208},{176,144},{112,80},{4... | collective-permute-start | bytes 1572872 | tf_op jit(solution)/shard_map/ppermute | solution.py:272
  45.7 32.5 %copy-start.3 = (f32[256,512]{1,0:T(8,128)}, f32[256,512]{1,0:T(8,128)S(1)}, u32[]{:S(2)}) copy-start(f32[256,512]{1,0:T(8,128)S(1)} %broadcast_select_fusion.rmine) | copy-start | bytes 1572868
  45.8 17.5 %collective-permute-start.8 = (f32[256,512]{1,0:T(8,128)S(1)}, f32[256,512]{1,0:T(8,128)S(1)}, u32[]{:S(2)}, u32[]{:S(2)}) collective-permute-start(f32[256,512]{1,0:T(8,128)S(1)} %broadcast_select_fusion.rmine), channel_id=1, source_target_pairs={{0,16},{16,0},{32,48},{48,32},{64,80},{80,64},{96,112},{112,96},{1... | collective-permute-start | bytes 1572872 | tf_op jit(solution)/shard_map/ppermute | solution.py:290
  45.9 27.1 %collective-permute-start.7 = (f32[512,256]{1,0:T(8,128)S(1)}, f32[512,256]{1,0:T(8,128)S(1)}, u32[]{:S(2)}, u32[]{:S(2)}) collective-permute-start(f32[512,256]{1,0:T(8,128)S(1)} %broadcast_select_fusion.8.mine.gmine), channel_id=1, source_target_pairs={{0,1},{1,0},{2,3},{3,2},{4,5},{5,4},{6,7},{7,6},{8,9},{9,8},{10,11... | collective-permute-start | bytes 1572872 | tf_op jit(solution)/shard_map/ppermute | solution.py:290
  58.3 14.6 %all-to-all-start.2 = ((f32[16,32,256]{2,1,0:T(8,128)}), f32[16,32,256]{2,1,0:T(8,128)S(1)}, u32[]{:S(2)}, u32[]{:S(2)}) async-start(f32[16,32,256]{2,1,0:T(8,128)} %bitcast.6), calls=%async_computation.2 | async-start | bytes 1048576 | tf_op jit(solution)/shard_map/all_to_all | solution.py:296
  61.9 1.4 collective-permute-start.13
  64.5 19.4 %collective-permute-start.14 = (f32[512,256]{1,0:T(8,128)S(1)}, f32[512,256]{1,0:T(8,128)}, u32[]{:S(2)}, u32[]{:S(2)}) collective-permute-start(f32[512,256]{1,0:T(8,128)S(1)} %maximum_select_fusion), channel_id=1, source_target_pairs={{0,8},{15,7},{16,24},{31,23},{32,40},{47,39},{48,56},{63,55},{64,7... | collective-permute-start | bytes 1572872 | tf_op jit(solution)/shard_map/ppermute | solution.py:272
  72.9 8.9 %collective-permute-start.9 = (f32[32,256]{1,0:T(8,128)S(1)}, f32[32,256]{1,0:T(8,128)S(1)}, u32[]{:S(2)}, u32[]{:S(2)}) collective-permute-start(f32[32,256]{1,0:T(8,128)S(1)} %reduce_sum.19), channel_id=1, source_target_pairs={{0,8},{15,7},{16,24},{31,23},{32,40},{47,39},{48,56},{63,55},{64,7... | collective-permute-start | bytes 98312 | tf_op jit(solution)/shard_map/ppermute | solution.py:272
  78.2 23.7 %all-to-all-start = ((f32[16,32,512]{2,1,0:T(8,128)}), f32[16,32,512]{2,1,0:T(8,128)S(1)}, u32[]{:S(2)}, u32[]{:S(2)}) async-start(f32[16,32,512]{2,1,0:T(8,128)} %bitcast.18), calls=%async_computation | async-start | bytes 2097152 | tf_op jit(solution)/shard_map/all_to_all | solution.py:296
  81.9 0.7 collective-permute-start.10
  82.6 15.6 %collective-permute-start.11 = (f32[32,256]{1,0:T(8,128)S(1)}, f32[32,256]{1,0:T(8,128)S(1)}, u32[]{:S(2)}, u32[]{:S(2)}) collective-permute-start(f32[32,256]{1,0:T(8,128)S(1)} %broadcast_select_fusion.10), channel_id=1, source_target_pairs={{0,2},{4,6},{8,10},{12,14},{15,13},{11,9},{7,5},{3,1},{16,18},{20,... | collective-permute-start | bytes 98312 | tf_op jit(solution)/shard_map/ppermute | solution.py:272
  84.0 25.9 %collective-permute-start.15 = (f32[512,256]{1,0:T(8,128)S(1)}, f32[512,256]{1,0:T(8,128)}, u32[]{:S(2)}, u32[]{:S(2)}) collective-permute-start(f32[512,256]{1,0:T(8,128)S(1)} %broadcast_select_fusion.3), channel_id=1, source_target_pairs={{0,4},{8,12},{15,11},{7,3},{16,20},{24,28},{31,27},{23,19},{32,36}... | collective-permute-start | bytes 1572872 | tf_op jit(solution)/shard_map/ppermute | solution.py:272
  98.1 3.8 %collective-permute-start.12 = (f32[32,256]{1,0:T(8,128)S(1)}, f32[32,256]{1,0:T(8,128)S(1)}, u32[]{:S(2)}, u32[]{:S(2)}) collective-permute-start(f32[32,256]{1,0:T(8,128)S(1)} %broadcast_select_fusion.11), channel_id=1, source_target_pairs={{0,1},{1,0},{2,3},{3,2},{4,5},{5,4},{6,7},{7,6},{8,9},{9,8},{10,11... | collective-permute-start | bytes 98312 | tf_op jit(solution)/shard_map/ppermute | solution.py:290
  103.0 22.5 %all-to-all-start.3 = ((f32[16,32,512]{2,1,0:T(8,128)}), f32[16,32,512]{2,1,0:T(8,128)S(1)}, u32[]{:S(2)}, u32[]{:S(2)}) async-start(f32[16,32,512]{2,1,0:T(8,128)} %broadcast_in_dim.5), calls=%async_computation.3 | async-start | bytes 2097152 | tf_op jit(solution)/shard_map/all_to_all | solution.py:302
  110.0 21.3 %collective-permute-start.16 = (f32[512,256]{1,0:T(8,128)S(1)}, f32[512,256]{1,0:T(8,128)}, u32[]{:S(2)}, u32[]{:S(2)}) collective-permute-start(f32[512,256]{1,0:T(8,128)S(1)} %broadcast_select_fusion.5), channel_id=1, source_target_pairs={{0,2},{4,6},{8,10},{12,14},{15,13},{11,9},{7,5},{3,1},{16,18},{20,... | collective-permute-start | bytes 1572872 | tf_op jit(solution)/shard_map/ppermute | solution.py:272
  126.8 30.4 %all-to-all-start.1 = ((f32[16,32,512]{2,1,0:T(8,128)}), f32[16,32,512]{2,1,0:T(8,128)S(1)}, u32[]{:S(2)}, u32[]{:S(2)}) async-start(f32[16,32,512]{2,1,0:T(8,128)} %broadcast_in_dim.4), calls=%async_computation.1 | async-start | bytes 2097152 | tf_op jit(solution)/shard_map/all_to_all | solution.py:302
  132.4 2.8 %collective-permute-start.17 = (f32[512,256]{1,0:T(8,128)S(1)}, f32[512,256]{1,0:T(8,128)S(1)}, u32[]{:S(2)}, u32[]{:S(2)}) collective-permute-start(f32[512,256]{1,0:T(8,128)S(1)} %broadcast_select_fusion.7.smine), channel_id=1, source_target_pairs={{0,1},{1,0},{2,3},{3,2},{4,5},{5,4},{6,7},{7,6},{8,9},{9,8},{10,11... | collective-permute-start | bytes 1572872 | tf_op jit(solution)/shard_map/ppermute | solution.py:290
  142.0 11.9 %collective-permute-start.18 = (f32[256,256]{1,0:T(8,128)}, f32[256,256]{1,0:T(8,128)S(1)}, u32[]{:S(2)}, u32[]{:S(2)}) collective-permute-start(f32[256,256]{1,0:T(8,128)} %get-tuple-element.38.b_here), channel_id=1, source_target_pairs={{0,240},{1,241},{2,242},{3,243},{4,244},{5,245},{6,246},{7,247},{8... | collective-permute-start | bytes 786440 | tf_op jit(solution)/shard_map/ppermute | solution.py:393
  (10 other events, 89.9 us)

commit v2 on v1

v2 whole, which is shorter than its diff:
```python
import functools

import jax
import jax.numpy as jnp
from jax import lax
from jax.experimental import pallas as pl
from jax.experimental.pallas import tpu as pltpu
from jax.sharding import PartitionSpec as P

W = 256
LANES = 128
SUB = 8
ROWS = W * SUB
F32 = jnp.float32
DIAG_HINT = 20 * 10**9
MAIN_HINT = 100 * 10**9
CHAIN_HINT = 40 * 10**9
STEP_HINT = 25 * 10**9
LIGHT = 1000
SUMS_HINT = 3 * 10**8
ANY = pl.BlockSpec(memory_space=pl.ANY)
HBM = pl.BlockSpec(memory_space=pltpu.HBM)
VMEM = pl.BlockSpec(memory_space=pltpu.VMEM)
SMEM = pl.BlockSpec(memory_space=pltpu.SMEM)


def product(left, right):
    return jnp.dot(left, right, precision=lax.Precision.HIGHEST, preferred_element_type=F32)


def product_t(left, right):
    return lax.dot_general(
        left, right, (((0,), (0,)), ((), ())), precision=lax.Precision.HIGHEST, preferred_element_type=F32
    )


def product_nt(left, right):
    return lax.dot_general(
        left, right, (((1,), (1,)), ((), ())), precision=lax.Precision.HIGHEST, preferred_element_type=F32
    )


def masks(size):
    rows = lax.broadcasted_iota(jnp.int32, (size, size), 0)
    cols = lax.broadcasted_iota(jnp.int32, (size, size), 1)
    return rows >= cols, rows == cols


def tril(matrix):
    return jnp.where(masks(matrix.shape[0])[0], matrix, 0.0)


def lower_half(matrix):
    low, diag = masks(matrix.shape[0])
    return jnp.where(diag, 0.5 * matrix, jnp.where(low, matrix, 0.0))


def call(body, out_shape, in_specs, out_specs, scratch, flops, moved, alias=None, vmem=20):
    return pl.pallas_call(
        body,
        out_shape=out_shape,
        in_specs=in_specs,
        out_specs=out_specs,
        scratch_shapes=scratch,
        input_output_aliases=alias or {},
        compiler_params=pltpu.CompilerParams(vmem_limit_bytes=vmem * 1024 * 1024),
        cost_estimate=pl.CostEstimate(flops=flops, bytes_accessed=moved, transcendentals=0),
    )


def shape(*dims):
    return jax.ShapeDtypeStruct(dims, F32)


def piece_of(buf, first, rows, k):
    return buf[pl.ds(first * SUB + k, rows, stride=SUB), :]


def entry_kernel(pos, g, l, slab, piece, corner, gbuf, lbuf, cbuf, sems):
    odd_row = pos[2]
    odd_col = pos[3]
    first = pltpu.make_async_copy(g.at[pl.ds(2 * ROWS, 2 * ROWS)], gbuf, sems.at[0])
    first.start()
    start = pl.multiple_of((2 - odd_row) * ROWS, ROWS)
    second = pltpu.make_async_copy(l.at[pl.ds(start, ROWS)], lbuf, sems.at[1])
    second.start()
    third = pltpu.make_async_copy(g.at[pl.ds(ROWS, ROWS)], cbuf, sems.at[2])
    third.start()
    first.wait()
    for odd in range(2):

        @pl.when(odd_col == odd)
        def _():
            for h in range(2):
                slab[:, h * LANES : (h + 1) * LANES] = piece_of(gbuf, 0, 2 * W, 2 * (2 - odd) + h)

    second.wait()
    for k in range(4):
        piece[:, k * LANES : (k + 1) * LANES] = piece_of(lbuf, 0, W, k)
    third.wait()
    for h in range(2):
        corner[:, h * LANES : (h + 1) * LANES] = piece_of(cbuf, 0, W, 2 + h)


def unpack_kernel(pos, l, slab, corner, inside, fslab, own, lbuf, sem):
    odd_col = pos[3]
    first = pltpu.make_async_copy(l.at[pl.ds(2 * ROWS, 2 * ROWS)], lbuf, sem)
    first.start()
    first.wait()
    for odd in range(2):

        @pl.when(odd_col == odd)
        def _():
            for h in range(2):
                fslab[:, h * LANES : (h + 1) * LANES] = piece_of(lbuf, 0, 2 * W, 2 * (2 - odd) + h)

    for k in range(4):
        inside[:, k * LANES : (k + 1) * LANES] = piece_of(lbuf, 0, 2 * W, k)
    for h in range(2):
        own[W:, h * LANES : (h + 1) * LANES] = piece_of(lbuf, 0, W, 4 + h)
    own[:W] = jnp.where(pos[0] == 15, corner[...], slab[:W])


def pick(pos, axis, mine, other):
    odd = pos[2 + axis] == 1
    return jnp.where(odd, other, mine), jnp.where(odd, mine, other)


def live_rows(pos, value):
    rows = lax.broadcasted_iota(jnp.int32, value.shape, 0)
    return jnp.where((pos[0] == 0) & (rows < W), 0.0, value)


def diag_kernel(pos, sent, slab, fslab, piece, out):
    right = fslab[...]
    left = jnp.where(pos[3] == 1, sent[...], slab[...])
    for half, value in enumerate((left, slab[...])):
        result = product_t(live_rows(pos, value), right)
        for j in range(8):
            out[8 * half + j, :32] = result[32 * j : 32 * j + 32]
    for j in range(16):
        for h in range(2):
            out[j, 32 + 16 * h : 48 + 16 * h] = piece[16 * j : 16 * j + 16, h * W : (h + 1) * W]


def first_parts_kernel(parts, out, chunk):
    total = parts[0, :32]
    for i in range(1, 16):
        total = total + parts[i, :32]
    for h in range(2):
        lanes = slice(h * W, (h + 1) * W)
        for j in range(16):
            out[j, :16, lanes] = total[16 * h : 16 * h + 16]
            out[j, 16:, lanes] = parts[0, 48 + 8 * h : 56 + 8 * h]
        for k, source in enumerate((0, 15)):
            chunk[16 * k : 16 * k + 16, lanes] = parts[source, 32 + 16 * h : 48 + 16 * h]


def panel_row(panels, which):
    return panels[:, 32 + 16 * which : 48 + 16 * which, :].reshape(W, 2 * W)


def diag_sum(parts, half):
    return jnp.concatenate(
        [parts[8 * half + j, :16, h * W : (h + 1) * W] for j in range(8) for h in range(2)], axis=0
    )


def l3231_of(parts):
    return jnp.concatenate(
        [parts[j, 16:, h * W : (h + 1) * W] for j in range(16) for h in range(2)], axis=0
    )


def sums_kernel(pos, mine, other, inside, chunk, out):
    right = inside[...]
    for half, value in enumerate(pick(pos, 1, mine[...], other[...])):
        result = product_t(live_rows(pos, value), right)
        for j in range(8):
            out[8 * half + j, :32] = result[32 * j : 32 * j + 32]
    for j in range(16):
        out[j, 32:] = chunk[...]


def second_parts_kernel(parts, out):
    total = parts[0, :32]
    for i in range(1, 16):
        total = total + parts[i, :32]
    for i in range(16):
        out[i] = total


def bulk_kernel(pos, g, gmine, gother, panels, smine, sother, z, out, gbuf, abuf, b0, b1, sems):
    load = pltpu.make_async_copy(g.at[pl.ds(2 * ROWS, 2 * ROWS)], gbuf, sems.at[0])
    load.start()
    above = pltpu.make_async_copy(g.at[pl.ds(0, 2 * ROWS)], abuf, sems.at[1])
    above.start()
    g32, g31 = pick(pos, 1, gmine[...], gother[...])
    l3231 = jnp.where(pos[3] == 1, smine[W:], sother[W:])
    below0 = product(g32, z[0])
    b0[...] = below0
    below1 = product(g31 - product(below0, l3231), z[1])
    b1[...] = below1
    change = product(below0, panel_row(panels, 0)) + product(below1, panel_row(panels, 1))
    above.wait()
    rest = pltpu.make_async_copy(abuf, out.at[pl.ds(0, 2 * ROWS)], sems.at[1])
    rest.start()
    load.wait()
    for k in range(4):
        at = pl.ds(k, 2 * W, stride=SUB)
        gbuf[at, :] = gbuf[at, :] - change[:, k * LANES : (k + 1) * LANES]

    @pl.when(pos[1] == 15)
    def _():
        for h in range(2):
            gbuf[pl.ds(2 + h, 2 * W, stride=SUB), :] = b1[:, h * LANES : (h + 1) * LANES]

    @pl.when(pos[1] == 0)
    def _():
        for h in range(2):
            gbuf[pl.ds(4 + h, 2 * W, stride=SUB), :] = b0[:, h * LANES : (h + 1) * LANES]

    store = pltpu.make_async_copy(gbuf, out.at[pl.ds(2 * ROWS, 2 * ROWS)], sems.at[0])
    store.start()
    rest.wait()
    store.wait()


def corner_kernel(pos, parts, own, sent, z, out):
    row, col = pos[0], pos[1]
    out[W:] = l3231_of(parts)

    @pl.when((row == 0) & (col == 0))
    def _():
        dbar = tril(own[:W] - product_t(z[0], diag_sum(parts, 0)))
        inner = lower_half(product_t(tril(own[W:]), dbar))
        sym = product(product_t(z[0], inner), z[0])
        out[:W] = sym + sym.T

    @pl.when((row == 0) & (col == 15))
    def _():
        out[:W] = own[:W] - product_t(z[0], diag_sum(parts, 0))

    @pl.when((row == 15) & (col == 15))
    def _():
        t31 = product_t(z[0], diag_sum(parts, 0))
        out[:W] = own[:W] - product_t(z[1], diag_sum(parts, 1) - product_t(out[W:], t31))

    @pl.when(((row != 0) & (row != 15)) | ((col != 0) & (col != 15)) | ((row == 15) & (col == 0)))
    def _():
        out[:W] = sent[...]


def below_kernel(pos, smine, sother, z, out):
    @pl.when(pos[0] == 0)
    def _():
        small0, small1 = pick(pos, 1, smine[...], sother[...])
        out[...] = product(small1[:W] - product(small0[:W], small1[W:]), z[1])

    @pl.when(pos[0] != 0)
    def _():
        out[...] = jnp.zeros_like(out)


def rows_kernel(pos, g, sums, panels, smine, sother, b_here, b_sent, z, done, out, gbuf, sem):
    small0, small1 = pick(pos, 1, smine[...], sother[...])

    def finished_row(first, update, corner, extra):
        load = pltpu.make_async_copy(g.at[pl.ds(first * ROWS, ROWS)], gbuf, sem)
        load.start()
        change = update()
        load.wait()
        for k in range(4):
            at = pl.ds(k, W, stride=SUB)
            gbuf[at, :] = gbuf[at, :] - change[:, k * LANES : (k + 1) * LANES]

        @pl.when(pos[1] == 15)
        def _():
            for h in range(2):
                gbuf[pl.ds(2 + h, W, stride=SUB), :] = corner[:, h * LANES : (h + 1) * LANES]

        if extra is not None:

            @pl.when(pos[1] == 0)
            def _():
                for h in range(2):
                    gbuf[pl.ds(4 + h, W, stride=SUB), :] = extra[:, h * LANES : (h + 1) * LANES]

        store = pltpu.make_async_copy(gbuf, out.at[pl.ds(first * ROWS, ROWS)], sem)
        store.start()
        store.wait()

    @pl.when(pos[0] == 0)
    def _():
        sym0 = small0[:W]

        def update():
            return (
                product_t(z[0], sums[:W])
                + product(sym0, panel_row(panels, 0))
                + product(b_here[...], panel_row(panels, 1))
            )

        finished_row(2, update, b_here[...], lower_half(sym0))

    @pl.when(pos[0] == 15)
    def _():
        l3131, l3231 = small0[:W], small1[W:]
        dbar = tril(small1[:W] - product_t(b_sent[...], l3231))
        inner = lower_half(product_t(tril(l3131), dbar))
        sym1 = product(product_t(z[1], inner), z[1])
        sym1 = sym1 + sym1.T

        def update():
            mix = product(z[0], product(l3231, z[1]))
            return (
                product_t(z[1], sums[W:])
                - product_t(mix, sums[:W])
                + product_t(b_sent[...], panel_row(panels, 0))
                + product(sym1, panel_row(panels, 1))
            )

        finished_row(1, update, lower_half(sym1), None)


RING = [[(0, 7)], [(0, 2), (7, 5)], [(0, 1), (7, 6), (5, 4), (2, 3)]]


def choose_kernel(pos, moved, kept, out, *, targets):
    got = functools.reduce(jnp.logical_or, [pos[1] == t for t in targets])

    @pl.when(got)
    def _():
        out[...] = moved[...]

    @pl.when(jnp.logical_not(got))
    def _():
        out[...] = kept[...]


def tree_step(pos, value, step, weight):
    pairs = [(2 * s, 2 * t) for s, t in RING[step]]
    pairs = pairs + [(15 - s, 15 - t) for s, t in pairs]
    moved = lax.ppermute(value, "col", pairs)
    kernel = functools.partial(choose_kernel, targets=[t for _, t in pairs])
    return call(kernel, shape(*value.shape), [SMEM] + [VMEM] * 2, VMEM, [], weight, 4 * value.size)(pos, moved, value)


def flipped(value, axis, flip):
    return lax.ppermute(value, axis, [(i, i ^ flip) for i in range(lax.axis_size(axis))])


def after(value, *others):
    return lax.optimization_barrier((value, *others))[0]


def exchange(parts):
    return lax.all_to_all(parts, "row", 0, 0)


def per_device(factor, adjoint, diag_inverse):
    my_row = lax.axis_index("row")
    my_col = lax.axis_index("col")
    pos = jnp.stack([my_row, my_col, my_row // 8, my_col % 2]).astype(jnp.int32)
    g = adjoint.reshape(4 * ROWS, LANES)
    l = factor.reshape(4 * ROWS, LANES)
    z = diag_inverse
    dma = pltpu.SemaphoreType.DMA
    block = W * W * 4

    slab, piece, corner = call(
        entry_kernel,
        (shape(2 * W, W), shape(W, 2 * W), shape(W, W)),
        [SMEM, HBM, HBM],
        (VMEM,) * 3,
        [
            pltpu.VMEM((2 * ROWS, LANES), F32),
            pltpu.VMEM((ROWS, LANES), F32),
            pltpu.VMEM((ROWS, LANES), F32),
            dma((3,)),
        ],
        0,
        16 * block,
        vmem=60,
    )(pos, g, l)
    gmine = tree_step(pos, slab, 0, LIGHT)
    inside, fslab, own = call(
        unpack_kernel,
        (shape(2 * W, 2 * W), shape(2 * W, W), shape(2 * W, W)),
        [SMEM, HBM, VMEM, VMEM],
        (VMEM,) * 3,
        [pltpu.VMEM((2 * ROWS, LANES), F32), dma],
        0,
        16 * block,
    )(pos, l, slab, corner)
    gmine = after(gmine, fslab)
    sent = lax.ppermute(gmine, "col", [(14, 15)])
    gmine = tree_step(pos, gmine, 1, STEP_HINT)

    partial = call(
        diag_kernel, shape(16, 64, W), [SMEM] + [VMEM] * 4, VMEM, [], 8 * W**3, 12 * block
    )(pos, sent, slab, fslab, piece)
    parts = exchange(partial)
    gmine = after(gmine, partial)
    spread, chunk = call(
        first_parts_kernel,
        (shape(16, 24, 2 * W), shape(32, 2 * W)),
        [VMEM],
        (VMEM,) * 2,
        [],
        DIAG_HINT,
        10 * block,
    )(after(parts, gmine))
    gmine = tree_step(pos, gmine, 2, STEP_HINT)
    gother = flipped(after(gmine, spread), "col", 1)
    spread = exchange(spread)

    partial = call(
        sums_kernel, shape(16, 64, 2 * W), [SMEM] + [VMEM] * 4, VMEM, [], SUMS_HINT, 20 * block
    )(pos, gmine, gother, inside, chunk)
    panels = exchange(after(partial, spread))

    sent = lax.ppermute(after(piece[:, W:], gmine), "col", [(15, 0)])
    smine = call(
        corner_kernel, shape(2 * W, W), [SMEM] + [VMEM] * 4, VMEM, [], CHAIN_HINT, 12 * block
    )(pos, after(spread, partial), own, sent, z)
    for step in range(3):
        smine = tree_step(pos, smine, step, LIGHT)
    sother = flipped(smine, "col", 1)

    sums = call(
        second_parts_kernel, shape(16, 32, 2 * W), [VMEM], VMEM, [], MAIN_HINT, 8 * block
    )(panels)
    sums = exchange(sums).reshape(2 * W, 2 * W)

    out = call(
        bulk_kernel,
        shape(4 * ROWS, LANES),
        [SMEM, HBM] + [VMEM] * 6,
        HBM,
        [
            pltpu.VMEM((2 * ROWS, LANES), F32),
            pltpu.VMEM((2 * ROWS, LANES), F32),
            pltpu.VMEM((2 * W, W), F32),
            pltpu.VMEM((2 * W, W), F32),
            dma((2,)),
        ],
        30 * W**3,
        40 * block,
        vmem=57,
    )(pos, g, gmine, gother, panels, smine, sother, z)

    below_row = call(
        below_kernel, shape(W, W), [SMEM] + [VMEM] * 3, VMEM, [], 4 * W**3, 8 * block
    )(pos, smine, sother, z)
    below_sent = lax.ppermute(below_row, "row", [(0, 15)])
    out = call(
        rows_kernel,
        shape(4 * ROWS, LANES),
        [SMEM, HBM] + [VMEM] * 7 + [HBM],
        HBM,
        [pltpu.VMEM((ROWS, LANES), F32), dma],
        LIGHT,
        LIGHT,
        alias={9: 0},
        vmem=57,
    )(pos, g, sums, panels, smine, sother, below_row, below_sent, z, out)
    return out.reshape(adjoint.shape)


def solution(mesh):
    placed = (P(None, "row", None, None, "col", None), P(None, "row", None, None, "col", None), P())
    return jax.shard_map(
        per_device,
        mesh=mesh,
        in_specs=placed,
        out_specs=P(None, "row", None, None, "col", None),
        check_vma=False,
    )
```

time: 166 us -> 143 us (0.86)
  starting transfers between devices: 59 us -> 48.2 us
  waiting for transfers between devices: 55.4 us -> 45.5 us
  local copies, waits for them, and re-layouts: 5.66 us -> 13.2 us
  other arithmetic: 5.79 us -> 0.55 us
  Pallas kernels: 36.5 us -> 33.6 us
    ppermute x18 -> x10, starting transfers between devices: 36.5 us -> 15.1 us  [the longest x6 9.43 us: tree_step(): moved = lax.ppermute(value, 'col', pairs)]
    all_to_all x4, waiting for transfers between devices: 21.1 us -> 11.6 us  [exchange(): return lax.all_to_all(parts, 'row', 0, 0)]
    unnamed x22 -> x40, local copies, waits for them, and re-layouts: 3.35 us -> 12.5 us
    all_to_all x4, starting transfers between devices: 18.6 us -> 25.9 us  [exchange(): return lax.all_to_all(parts, 'row', 0, 0)]
    select_n x15 -> x0, other arithmetic: 5.04 us -> none  [the longest x12 3.84 us: tree_step(): return jnp.where(got, moved, value)]
    ppermute x1, starting transfers between devices: 3.94 us -> 7.24 us  [per_device(): below_sent = lax.ppermute(below_row, 'row', [(0, 15)])]
    pallas_call x8 -> x16, Pallas kernels: 36.5 us -> 33.6 us  [the longest x1 8.21 us: per_device(): call(bulk_kernel, shape(4 * ROWS, LANES), [SMEM, HBM] + [VMEM] * 6, HBM,...]
    broadcast_in_dim x2 -> x0, local copies, waits for them, and re-layouts: 2.31 us -> none  [gather_parts(): parts = jnp.broadcast_to(part[None], (size,) + part.shape)]
  transfers between devices with their start and end apart: 23 -> 15, of which waited for: 7 -> 6; matrix products, arithmetic and copies ran while one was open for 4% -> 1% of each run, Pallas kernels for 17% -> 17%
where the time goes in v2:
time: 143 us; the launch traced here: 142 us
  starting transfers between devices  48.2 us (34%)
  waiting for transfers between devices  45.5 us (32%)
  Pallas kernels  33.6 us (23%)
  local copies, waits for them, and re-layouts  13.2 us (9%)
    ppermute x6, waiting for transfers between devices, tree_step(): moved = lax.ppermute(value, 'col', pairs)  32.2 us
    all_to_all x4, starting transfers between devices, exchange(): return lax.all_to_all(parts, 'row', 0, 0)  25.9 us
    unnamed x40, local copies, waits for them, and re-layouts  12.5 us
    all_to_all x4, waiting for transfers between devices, exchange(): return lax.all_to_all(parts, 'row', 0, 0)  11.6 us
    ppermute x6, starting transfers between devices, tree_step(): moved = lax.ppermute(value, 'col', pairs)  9.43 us
    pallas_call x1, Pallas kernels, per_device(): call(bulk_kernel, shape(4 * ROWS, LANES), [SMEM, HBM] + [VMEM] * 6, HBM,...  8.21 us
    ppermute x1, starting transfers between devices, per_device(): below_sent = lax.ppermute(below_row, 'row', [(0, 15)])  7.24 us
    pallas_call x6, Pallas kernels, tree_step(): call(kernel, shape(*value.shape), [SMEM] + [VMEM] * 2, VMEM, [], weight,...  5.84 us
  transfers between devices with their start and end apart: 15, of which 6 were waited for; matrix products, arithmetic and copies ran while one was open for 1% of the time, Pallas kernels for 17%

profile of v2, /device:TPU:1, one launch (start us, length us, event | category | flops | bytes accessed | tf_op | source)
XLA Modules:
  0.0 141.6 jit_solution(4096216125886009979)
XLA Ops:
  0.6 4.0 %shard_map.37 = (f32[512,256]{1,0:T(8,128)}, f32[256,512]{1,0:T(8,128)}, f32[256,256]{1,0:T(8,128)}) custom-call(s32[4]{0:T(128)} %pad_add_fusion.pos, f32[8192,128]{1,0:T(8,128)} %bitcast.10, f32[8192,128]{1,0:T(8,128)} %bitcast.8), custom_call_target="tpu_custom_call" | custom-call | bytes 4194304 | tf_op jit(solution)/shard_map/pallas_call | solution.py:371
  5.9 2.2 %copy-done.1 = f32[4,1,256,4,1,256]{5,4,3,2,1,0:T(1,128)S(1)} copy-done((f32[4,1,256,4,1,256]{5,4,3,2,1,0:T(1,128)S(1)}, f32[4,1,256,4,1,256]{5,4,3,2,1,0:T(1,128)}, u32[]{:S(2)}) %copy-start.1) | copy-done | bytes 4194328
  11.3 7.8 %collective-permute-done.moved = f32[512,256]{1,0:T(8,128)S(1)} collective-permute-done((f32[512,256]{1,0:T(8,128)}, f32[512,256]{1,0:T(8,128)S(1)}, u32[]{:S(2)}, u32[]{:S(2)}) %collective-permute-start) | collective-permute-done | bytes 524320 | tf_op jit(solution)/shard_map/ppermute | solution.py:344
  20.4 2.1 %collective-permute-start.1 = (f32[512,256]{1,0:T(8,128)S(1)}, f32[512,256]{1,0:T(8,128)}, u32[]{:S(2)}, u32[]{:S(2)}) collective-permute-start(f32[512,256]{1,0:T(8,128)S(1)} %shard_map.38.kept), channel_id=1, source_target_pairs={{0,4},{14,10},{15,11},{1,5},{16,20},{30,26},{31,27},{17,21},{32,36... | collective-permute-start | bytes 1572872 | tf_op jit(solution)/shard_map/ppermute | solution.py:344
  22.5 2.7 %shard_map.41 = f32[16,64,256]{2,1,0:T(8,128)} custom-call(s32[4]{0:T(128)S(1)} %copy-done.13, f32[512,256]{1,0:T(8,128)S(1)} %collective-permute-done.2.sent, f32[512,256]{1,0:T(8,128)S(1)} %copy-done.6, f32[512,256]{1,0:T(8,128)S(1)} %get-tuple-element.22.fslab, f32[256,512]{1,0:T(8,128)S(1)} %copy-done.9), custom_call_target="tpu_custom_call" | custom-call | flops 134217728 | bytes 3145728 | tf_op jit(solution)/shard_map/pallas_call | solution.py:400
  25.2 6.8 %all-to-all-start = ((f32[16,64,256]{2,1,0:T(8,128)}), f32[16,64,256]{2,1,0:T(8,128)S(1)}, u32[]{:S(2)}, u32[]{:S(2)}) async-start(f32[16,64,256]{2,1,0:T(8,128)} %shard_map.41), calls=%async_computation | async-start | bytes 2097152 | tf_op jit(solution)/shard_map/all_to_all | solution.py:358
  31.9 1.9 %shard_map.40.kept = f32[512,256]{1,0:T(8,128)} custom-call(s32[4]{0:T(128)S(1)} %copy-done.13, f32[512,256]{1,0:T(8,128)} %collective-permute-done.1.moved, f32[512,256]{1,0:T(8,128)S(1)} %shard_map.38.kept), custom_call_target="tpu_custom_call" | custom-call | flops 24999999488 | bytes 524288 | tf_op jit(solution)/shard_map/pallas_call | solution.py:346
  33.8 1.3 collective-permute-start.3
  35.2 11.6 %all-to-all-done.parts = f32[16,64,256]{2,1,0:T(8,128)S(1)} async-done(((f32[16,64,256]{2,1,0:T(8,128)}), f32[16,64,256]{2,1,0:T(8,128)S(1)}, u32[]{:S(2)}, u32[]{:S(2)}) %all-to-all-start) | async-done | bytes 1048608 | tf_op jit(solution)/shard_map/all_to_all | solution.py:358
  47.7 4.6 %all-to-all-start.1 = ((f32[16,24,512]{2,1,0:T(8,128)}), f32[16,24,512]{2,1,0:T(8,128)}, u32[]{:S(2)}, u32[]{:S(2)}) async-start(f32[16,24,512]{2,1,0:T(8,128)} %get-tuple-element.27), calls=%async_computation.1 | async-start | bytes 1572864 | tf_op jit(solution)/shard_map/all_to_all | solution.py:358
  55.3 3.0 %collective-permute-start.4 = (f32[512,256]{1,0:T(8,128)S(1)}, f32[512,256]{1,0:T(8,128)S(1)}, u32[]{:S(2)}, u32[]{:S(2)}) collective-permute-start(f32[512,256]{1,0:T(8,128)S(1)} %shard_map.42.mine.gmine), channel_id=1, source_target_pairs={{0,1},{1,0},{2,3},{3,2},{4,5},{5,4},{6,7},{7,6},{8,9},{9,8},{10,11... | collective-permute-start | bytes 1572872 | tf_op jit(solution)/shard_map/ppermute | solution.py:350
  59.9 2.5 %shard_map.44 = f32[16,64,512]{2,1,0:T(8,128)S(1)} custom-call(s32[4]{0:T(128)S(1)} %copy-done.13, f32[512,256]{1,0:T(8,128)S(1)} %shard_map.42.mine.gmine, f32[512,256]{1,0:T(8,128)S(1)} %collective-permute-done.4.other.gother, f32[512,512]{1,0:T(8,128)S(1)} %get-tuple-element.29.inside, f32[32,512]{1,0:T(8,128)S(1)} %get-tuple-element.30.chunk), custom_call_target="tpu_custom_call" | custom-call | flops 300000000 | bytes 5242880 | tf_op jit(solution)/shard_map/pallas_call | solution.py:418
  64.5 6.8 %all-to-all-start.2 = ((f32[16,64,512]{2,1,0:T(8,128)}), f32[16,64,512]{2,1,0:T(8,128)S(1)}, u32[]{:S(2)}, u32[]{:S(2)}) async-start(f32[16,64,512]{2,1,0:T(8,128)} %copy-done.3), calls=%async_computation.2 | async-start | bytes 4194304 | tf_op jit(solution)/shard_map/all_to_all | solution.py:358
  74.9 13.3 %collective-permute-done.6.moved = f32[512,256]{1,0:T(8,128)S(1)} collective-permute-done((f32[512,256]{1,0:T(8,128)S(1)}, f32[512,256]{1,0:T(8,128)S(1)}, u32[]{:S(2)}, u32[]{:S(2)}) %collective-permute-start.6) | collective-permute-done | bytes 524320 | tf_op jit(solution)/shard_map/ppermute | solution.py:344
  88.7 1.3 collective-permute-start.7
  90.1 11.1 %collective-permute-done.7.moved = f32[512,256]{1,0:T(8,128)S(1)} collective-permute-done((f32[512,256]{1,0:T(8,128)S(1)}, f32[512,256]{1,0:T(8,128)S(1)}, u32[]{:S(2)}, u32[]{:S(2)}) %collective-permute-start.7) | collective-permute-done | bytes 524320 | tf_op jit(solution)/shard_map/ppermute | solution.py:344
  101.7 2.1 %collective-permute-start.8 = (f32[512,256]{1,0:T(8,128)S(1)}, f32[512,256]{1,0:T(8,128)}, u32[]{:S(2)}, u32[]{:S(2)}) collective-permute-start(f32[512,256]{1,0:T(8,128)S(1)} %shard_map.48.kept), channel_id=1, source_target_pairs={{0,2},{14,12},{10,8},{4,6},{15,13},{1,3},{5,7},{11,9},{16,18},{30,... | collective-permute-start | bytes 1572872 | tf_op jit(solution)/shard_map/ppermute | solution.py:344
  106.2 7.7 %all-to-all-start.3 = ((f32[16,32,512]{2,1,0:T(8,128)}), f32[16,32,512]{2,1,0:T(8,128)S(1)}, u32[]{:S(2)}, u32[]{:S(2)}) async-start(f32[16,32,512]{2,1,0:T(8,128)} %copy-done.11), calls=%async_computation.3 | async-start | bytes 2097152 | tf_op jit(solution)/shard_map/all_to_all | solution.py:358
  115.0 1.3 collective-permute-start.9
  116.4 1.5 %collective-permute-done.9.sother = f32[512,256]{1,0:T(8,128)S(1)} collective-permute-done((f32[512,256]{1,0:T(8,128)S(1)}, f32[512,256]{1,0:T(8,128)S(1)}, u32[]{:S(2)}, u32[]{:S(2)}) %collective-permute-start.9) | collective-permute-done | bytes 524320 | tf_op jit(solution)/shard_map/ppermute | solution.py:350
  117.9 1.8 %shard_map.50.b_here = f32[256,256]{1,0:T(8,128)S(1)} custom-call(s32[4]{0:T(128)S(1)} %copy-done.13, f32[512,256]{1,0:T(8,128)S(1)} %shard_map.49.smine, f32[512,256]{1,0:T(8,128)S(1)} %collective-permute-done.9.sother, f32[2,256,256]{2,1,0:T(8,128)S(1)} %copy-done.4), custom_call_target="tpu_custom_call" | custom-call | flops 67108864 | bytes 2097152 | tf_op jit(solution)/shard_map/pallas_call | solution.py:453
  119.7 7.2 %collective-permute-start.10 = (f32[256,256]{1,0:T(8,128)S(1)}, f32[256,256]{1,0:T(8,128)S(1)}, u32[]{:S(2)}, u32[]{:S(2)}) collective-permute-start(f32[256,256]{1,0:T(8,128)S(1)} %shard_map.50.b_here), channel_id=1, source_target_pairs={{0,240},{1,241},{2,242},{3,243},{4,244},{5,245},{6,246},{7,247},{8... | collective-permute-start | bytes 786440 | tf_op jit(solution)/shard_map/ppermute | solution.py:456
  127.0 8.2 %shard_map.51.done = f32[8192,128]{1,0:T(8,128)} custom-call(s32[4]{0:T(128)} %pad_add_fusion.pos, f32[8192,128]{1,0:T(8,128)} %bitcast.11, f32[512,256]{1,0:T(8,128)} %copy-done.7, f32[512,256]{1,0:T(8,128)} %copy-done.8, f32[16,64,512]{2,1,0:T(8,128)} %copy-done, f32[512,256]{1,0:T(8,128)} %copy-done.2, f32[512,256]{1,0:T(8,128)} %copy-done.5, ...), custom_call_target="tpu_custom_call" | custom-call | flops 503316480 | bytes 10485760 | tf_op jit(solution)/shard_map/pallas_call | solution.py:436
  136.3 5.1 %shard_map.52 = f32[8192,128]{1,0:T(8,128)} custom-call(s32[4]{0:T(128)} %pad_add_fusion.pos, f32[8192,128]{1,0:T(8,128)} %bitcast.12, f32[512,512]{1,0:T(8,128)} %bitcast.13, f32[16,64,512]{2,1,0:T(8,128)} %copy-done, f32[512,256]{1,0:T(8,128)} %copy-done.2, f32[512,256]{1,0:T(8,128)} %copy-done.5, ...), custom_call_target="tpu_custom_call", output_to_operand_aliasing={{}: (9, {})} | custom-call | flops 1000 | bytes 1000 | tf_op jit(solution)/shard_map/pallas_call | solution.py:457
  (64 shorter events, 23.0 us)
Async XLA Ops:
  0.6 5.4 %copy-start.13 = (s32[4]{0:T(128)S(1)}, s32[4]{0:T(128)}, u32[]{:S(2)}) copy-start(s32[4]{0:T(128)} %pad_add_fusion.pos) | copy-start | bytes 52
  4.6 14.5 %collective-permute-start = (f32[512,256]{1,0:T(8,128)}, f32[512,256]{1,0:T(8,128)S(1)}, u32[]{:S(2)}, u32[]{:S(2)}) collective-permute-start(f32[512,256]{1,0:T(8,128)} %get-tuple-element.20.kept.slab), channel_id=1, source_target_pairs={{0,14},{15,1},{16,30},{31,17},{32,46},{47,33},{48,62},{63,49},{64,... | collective-permute-start | bytes 1572872 | tf_op jit(solution)/shard_map/ppermute | solution.py:344
  5.9 2.2 %copy-start.1 = (f32[4,1,256,4,1,256]{5,4,3,2,1,0:T(1,128)S(1)}, f32[4,1,256,4,1,256]{5,4,3,2,1,0:T(1,128)}, u32[]{:S(2)}) copy-start(f32[4,1,256,4,1,256]{5,4,3,2,1,0:T(1,128)} %param.3) | copy-start | bytes 12582916
  10.1 12.4 %copy-start.9 = (f32[256,512]{1,0:T(8,128)S(1)}, f32[256,512]{1,0:T(8,128)}, u32[]{:S(2)}) copy-start(f32[256,512]{1,0:T(8,128)} %get-tuple-element.24.piece) | copy-start | bytes 1572868
  11.2 11.2 %copy-start.14 = (f32[512,256]{1,0:T(8,128)}, f32[512,256]{1,0:T(8,128)S(1)}, u32[]{:S(2)}) copy-start(f32[512,256]{1,0:T(8,128)S(1)} %get-tuple-element.33.own) | copy-start | bytes 1572868
  19.7 2.8 %collective-permute-start.2 = (f32[512,256]{1,0:T(8,128)S(1)}, f32[512,256]{1,0:T(8,128)S(1)}, u32[]{:S(2)}, u32[]{:S(2)}) collective-permute-start(f32[512,256]{1,0:T(8,128)S(1)} %shard_map.38.kept), channel_id=1, source_target_pairs={{14,15},{30,31},{46,47},{62,63},{78,79},{94,95},{110,111},{126,127... | collective-permute-start | bytes 1572872 | tf_op jit(solution)/shard_map/ppermute | solution.py:397
  20.4 11.6 %collective-permute-start.1 = (f32[512,256]{1,0:T(8,128)S(1)}, f32[512,256]{1,0:T(8,128)}, u32[]{:S(2)}, u32[]{:S(2)}) collective-permute-start(f32[512,256]{1,0:T(8,128)S(1)} %shard_map.38.kept), channel_id=1, source_target_pairs={{0,4},{14,10},{15,11},{1,5},{16,20},{30,26},{31,27},{17,21},{32,36... | collective-permute-start | bytes 1572872 | tf_op jit(solution)/shard_map/ppermute | solution.py:344
  25.2 21.6 %all-to-all-start = ((f32[16,64,256]{2,1,0:T(8,128)}), f32[16,64,256]{2,1,0:T(8,128)S(1)}, u32[]{:S(2)}, u32[]{:S(2)}) async-start(f32[16,64,256]{2,1,0:T(8,128)} %shard_map.41), calls=%async_computation | async-start | bytes 2097152 | tf_op jit(solution)/shard_map/all_to_all | solution.py:358
  33.8 18.6 %collective-permute-start.3 = (f32[512,256]{1,0:T(8,128)}, f32[512,256]{1,0:T(8,128)S(1)}, u32[]{:S(2)}, u32[]{:S(2)}) collective-permute-start(f32[512,256]{1,0:T(8,128)} %shard_map.40.kept), channel_id=1, source_target_pairs={{0,2},{14,12},{10,8},{4,6},{15,13},{1,3},{5,7},{11,9},{16,18},{30,... | collective-permute-start | bytes 1572872 | tf_op jit(solution)/shard_map/ppermute | solution.py:344
  47.7 16.8 %all-to-all-start.1 = ((f32[16,24,512]{2,1,0:T(8,128)}), f32[16,24,512]{2,1,0:T(8,128)}, u32[]{:S(2)}, u32[]{:S(2)}) async-start(f32[16,24,512]{2,1,0:T(8,128)} %get-tuple-element.27), calls=%async_computation.1 | async-start | bytes 1572864 | tf_op jit(solution)/shard_map/all_to_all | solution.py:358
  55.3 9.2 %copy-start.7 = (f32[512,256]{1,0:T(8,128)}, f32[512,256]{1,0:T(8,128)S(1)}, u32[]{:S(2)}) copy-start(f32[512,256]{1,0:T(8,128)S(1)} %shard_map.42.mine.gmine) | copy-start | bytes 1572868
  55.3 4.5 %collective-permute-start.4 = (f32[512,256]{1,0:T(8,128)S(1)}, f32[512,256]{1,0:T(8,128)S(1)}, u32[]{:S(2)}, u32[]{:S(2)}) collective-permute-start(f32[512,256]{1,0:T(8,128)S(1)} %shard_map.42.mine.gmine), channel_id=1, source_target_pairs={{0,1},{1,0},{2,3},{3,2},{4,5},{5,4},{6,7},{7,6},{8,9},{9,8},{10,11... | collective-permute-start | bytes 1572872 | tf_op jit(solution)/shard_map/ppermute | solution.py:350
  59.0 12.3 %collective-permute-start.5 = (f32[256,256]{1,0:T(8,128)}, f32[256,256]{1,0:T(8,128)S(1)}, u32[]{:S(2)}, u32[]{:S(2)}) collective-permute-start(f32[256,256]{1,0:T(8,128)} %slice.3), channel_id=1, source_target_pairs={{15,0},{31,16},{47,32},{63,48},{79,64},{95,80},{111,96},{127,112},... | collective-permute-start | bytes 786440 | tf_op jit(solution)/shard_map/ppermute | solution.py:423
  59.9 11.5 %copy-start.4 = (f32[2,256,256]{2,1,0:T(8,128)S(1)}, f32[2,256,256]{2,1,0:T(8,128)}, u32[]{:S(2)}) copy-start(f32[2,256,256]{2,1,0:T(8,128)} %z.7) | copy-start | bytes 1572868
  64.5 39.3 %all-to-all-start.2 = ((f32[16,64,512]{2,1,0:T(8,128)}), f32[16,64,512]{2,1,0:T(8,128)S(1)}, u32[]{:S(2)}, u32[]{:S(2)}) async-start(f32[16,64,512]{2,1,0:T(8,128)} %copy-done.3), calls=%async_computation.2 | async-start | bytes 4194304 | tf_op jit(solution)/shard_map/all_to_all | solution.py:358
  73.6 14.6 %collective-permute-start.6 = (f32[512,256]{1,0:T(8,128)S(1)}, f32[512,256]{1,0:T(8,128)S(1)}, u32[]{:S(2)}, u32[]{:S(2)}) collective-permute-start(f32[512,256]{1,0:T(8,128)S(1)} %shard_map.46.kept), channel_id=1, source_target_pairs={{0,14},{15,1},{16,30},{31,17},{32,46},{47,33},{48,62},{63,49},{64,... | collective-permute-start | bytes 1572872 | tf_op jit(solution)/shard_map/ppermute | solution.py:344
  88.7 12.4 %collective-permute-start.7 = (f32[512,256]{1,0:T(8,128)S(1)}, f32[512,256]{1,0:T(8,128)S(1)}, u32[]{:S(2)}, u32[]{:S(2)}) collective-permute-start(f32[512,256]{1,0:T(8,128)S(1)} %shard_map.47.kept), channel_id=1, source_target_pairs={{0,4},{14,10},{15,11},{1,5},{16,20},{30,26},{31,27},{17,21},{32,36... | collective-permute-start | bytes 1572872 | tf_op jit(solution)/shard_map/ppermute | solution.py:344
  101.7 12.2 %collective-permute-start.8 = (f32[512,256]{1,0:T(8,128)S(1)}, f32[512,256]{1,0:T(8,128)}, u32[]{:S(2)}, u32[]{:S(2)}) collective-permute-start(f32[512,256]{1,0:T(8,128)S(1)} %shard_map.48.kept), channel_id=1, source_target_pairs={{0,2},{14,12},{10,8},{4,6},{15,13},{1,3},{5,7},{11,9},{16,18},{30,... | collective-permute-start | bytes 1572872 | tf_op jit(solution)/shard_map/ppermute | solution.py:344
  106.2 29.0 %all-to-all-start.3 = ((f32[16,32,512]{2,1,0:T(8,128)}), f32[16,32,512]{2,1,0:T(8,128)S(1)}, u32[]{:S(2)}, u32[]{:S(2)}) async-start(f32[16,32,512]{2,1,0:T(8,128)} %copy-done.11), calls=%async_computation.3 | async-start | bytes 2097152 | tf_op jit(solution)/shard_map/all_to_all | solution.py:358
  115.0 11.9 %copy-start.2 = (f32[512,256]{1,0:T(8,128)}, f32[512,256]{1,0:T(8,128)S(1)}, u32[]{:S(2)}) copy-start(f32[512,256]{1,0:T(8,128)S(1)} %shard_map.49.smine) | copy-start | bytes 1572868
  115.0 2.9 %collective-permute-start.9 = (f32[512,256]{1,0:T(8,128)S(1)}, f32[512,256]{1,0:T(8,128)S(1)}, u32[]{:S(2)}, u32[]{:S(2)}) collective-permute-start(f32[512,256]{1,0:T(8,128)S(1)} %shard_map.49.smine), channel_id=1, source_target_pairs={{0,1},{1,0},{2,3},{3,2},{4,5},{5,4},{6,7},{7,6},{8,9},{9,8},{10,11... | collective-permute-start | bytes 1572872 | tf_op jit(solution)/shard_map/ppermute | solution.py:350
  117.9 9.0 %copy-start.5 = (f32[512,256]{1,0:T(8,128)}, f32[512,256]{1,0:T(8,128)S(1)}, u32[]{:S(2)}) copy-start(f32[512,256]{1,0:T(8,128)S(1)} %collective-permute-done.9.sother) | copy-start | bytes 1572868
  119.7 15.5 %copy-start.10 = (f32[256,256]{1,0:T(8,128)}, f32[256,256]{1,0:T(8,128)S(1)}, u32[]{:S(2)}) copy-start(f32[256,256]{1,0:T(8,128)S(1)} %shard_map.50.b_here) | copy-start | bytes 786436
  119.7 15.5 %collective-permute-start.10 = (f32[256,256]{1,0:T(8,128)S(1)}, f32[256,256]{1,0:T(8,128)S(1)}, u32[]{:S(2)}, u32[]{:S(2)}) collective-permute-start(f32[256,256]{1,0:T(8,128)S(1)} %shard_map.50.b_here), channel_id=1, source_target_pairs={{0,240},{1,241},{2,242},{3,243},{4,244},{5,245},{6,246},{7,247},{8... | collective-permute-start | bytes 786440 | tf_op jit(solution)/shard_map/ppermute | solution.py:456
  (11 other events, 11.1 us)

commit v3 on v2

--- a/solution.py
+++ b/solution.py
@@ -76,17 +76,11 @@
     return buf[pl.ds(first * SUB + k, rows, stride=SUB), :]
 
 
-def entry_kernel(pos, g, l, slab, piece, corner, gbuf, lbuf, cbuf, sems):
-    odd_row = pos[2]
-    odd_col = pos[3]
-    first = pltpu.make_async_copy(g.at[pl.ds(2 * ROWS, 2 * ROWS)], gbuf, sems.at[0])
-    first.start()
-    start = pl.multiple_of((2 - odd_row) * ROWS, ROWS)
-    second = pltpu.make_async_copy(l.at[pl.ds(start, ROWS)], lbuf, sems.at[1])
-    second.start()
-    third = pltpu.make_async_copy(g.at[pl.ds(ROWS, ROWS)], cbuf, sems.at[2])
-    third.start()
-    first.wait()
+def entry_kernel(g, slab, gbuf, sem):
+    load = pltpu.make_async_copy(g.at[pl.ds(2 * ROWS, 2 * ROWS)], gbuf, sem)
+    load.start()
+    odd_col = lax.axis_index("col") % 2
+    load.wait()
     for odd in range(2):
 
         @pl.when(odd_col == odd)
@@ -94,18 +88,16 @@
             for h in range(2):
                 slab[:, h * LANES : (h + 1) * LANES] = piece_of(gbuf, 0, 2 * W, 2 * (2 - odd) + h)
 
-    second.wait()
-    for k in range(4):
-        piece[:, k * LANES : (k + 1) * LANES] = piece_of(lbuf, 0, W, k)
-    third.wait()
-    for h in range(2):
-        corner[:, h * LANES : (h + 1) * LANES] = piece_of(cbuf, 0, W, 2 + h)
-
-
-def unpack_kernel(pos, l, slab, corner, inside, fslab, own, lbuf, sem):
+
+def unpack_kernel(pos, g, l, slab, inside, fslab, piece, own, lbuf, pbuf, gbuf, sems):
     odd_col = pos[3]
-    first = pltpu.make_async_copy(l.at[pl.ds(2 * ROWS, 2 * ROWS)], lbuf, sem)
+    first = pltpu.make_async_copy(l.at[pl.ds(2 * ROWS, 2 * ROWS)], lbuf, sems.at[0])
     first.start()
+    start = pl.multiple_of((2 - pos[2]) * ROWS, ROWS)
+    second = pltpu.make_async_copy(l.at[pl.ds(start, ROWS)], pbuf, sems.at[1])
+    second.start()
+    third = pltpu.make_async_copy(g.at[pl.ds(ROWS, ROWS)], gbuf, sems.at[2])
+    third.start()
     first.wait()
     for odd in range(2):
 
@@ -118,7 +110,19 @@
         inside[:, k * LANES : (k + 1) * LANES] = piece_of(lbuf, 0, 2 * W, k)
     for h in range(2):
         own[W:, h * LANES : (h + 1) * LANES] = piece_of(lbuf, 0, W, 4 + h)
-    own[:W] = jnp.where(pos[0] == 15, corner[...], slab[:W])
+    second.wait()
+    for k in range(4):
+        piece[:, k * LANES : (k + 1) * LANES] = piece_of(pbuf, 0, W, k)
+    third.wait()
+
+    @pl.when(pos[0] == 15)
+    def _():
+        for h in range(2):
+            own[:W, h * LANES : (h + 1) * LANES] = piece_of(gbuf, 0, W, 2 + h)
+
+    @pl.when(pos[0] != 15)
+    def _():
+        own[:W] = slab[:W]
 
 
 def pick(pos, axis, mine, other):
@@ -262,7 +266,24 @@
         out[...] = jnp.zeros_like(out)
 
 
-def rows_kernel(pos, g, sums, panels, smine, sother, b_here, b_sent, z, done, out, gbuf, sem):
+def ready_kernel(pos, sums, panels, smine, sother, b_here, z, out):
+    @pl.when(pos[0] == 0)
+    def _():
+        sym0 = jnp.where(pos[3] == 1, sother[:W], smine[:W])
+        out[...] = (
+            product_t(z[0], sums[:W])
+            + product(sym0, panel_row(panels, 0))
+            + product(b_here[...], panel_row(panels, 1))
+        )
+
+    @pl.when(pos[0] == 15)
+    def _():
+        l3231 = jnp.where(pos[3] == 1, smine[W:], sother[W:])
+        mix = product(z[0], product(l3231, z[1]))
+        out[...] = product_t(z[1], sums[W:]) - product_t(mix, sums[:W])
+
+
+def rows_kernel(pos, g, ready, panels, smine, sother, b_here, b_sent, z, done, out, gbuf, sem):
     small0, small1 = pick(pos, 1, smine[...], sother[...])
 
     def finished_row(first, update, corner, extra):
@@ -292,33 +313,18 @@
 
     @pl.when(pos[0] == 0)
     def _():
-        sym0 = small0[:W]
-
-        def update():
-            return (
-                product_t(z[0], sums[:W])
-                + product(sym0, panel_row(panels, 0))
-                + product(b_here[...], panel_row(panels, 1))
-            )
-
-        finished_row(2, update, b_here[...], lower_half(sym0))
+        finished_row(2, lambda: ready[...], b_here[...], lower_half(small0[:W]))
 
     @pl.when(pos[0] == 15)
     def _():
-        l3131, l3231 = small0[:W], small1[W:]
-        dbar = tril(small1[:W] - product_t(b_sent[...], l3231))
-        inner = lower_half(product_t(tril(l3131), dbar))
+        below = b_sent[...]
+        dbar = tril(small1[:W] - product_t(below, small1[W:]))
+        inner = lower_half(product_t(tril(small0[:W]), dbar))
         sym1 = product(product_t(z[1], inner), z[1])
         sym1 = sym1 + sym1.T
 
         def update():
-            mix = product(z[0], product(l3231, z[1]))
-            return (
-                product_t(z[1], sums[W:])
-                - product_t(mix, sums[:W])
-                + product_t(b_sent[...], panel_row(panels, 0))
-                + product(sym1, panel_row(panels, 1))
-            )
+            return ready[...] + product_t(below, panel_row(panels, 0)) + product(sym1, panel_row(panels, 1))
 
         finished_row(1, update, lower_half(sym1), None)
 
@@ -368,11 +374,22 @@
     dma = pltpu.SemaphoreType.DMA
     block = W * W * 4
 
-    slab, piece, corner = call(
+    slab = call(
         entry_kernel,
-        (shape(2 * W, W), shape(W, 2 * W), shape(W, W)),
-        [SMEM, HBM, HBM],
-        (VMEM,) * 3,
+        shape(2 * W, W),
+        [HBM],
+        VMEM,
+        [pltpu.VMEM((2 * ROWS, LANES), F32), dma],
+        0,
+        10 * block,
+        vmem=60,
+    )(g)
+    gmine = tree_step(pos, slab, 0, LIGHT)
+    inside, fslab, piece, own = call(
+        unpack_kernel,
+        (shape(2 * W, 2 * W), shape(2 * W, W), shape(W, 2 * W), shape(2 * W, W)),
+        [SMEM, HBM, HBM, VMEM],
+        (VMEM,) * 4,
         [
             pltpu.VMEM((2 * ROWS, LANES), F32),
             pltpu.VMEM((ROWS, LANES), F32),
@@ -380,19 +397,9 @@
             dma((3,)),
         ],
         0,
-        16 * block,
-        vmem=60,
-    )(pos, g, l)
-    gmine = tree_step(pos, slab, 0, LIGHT)
-    inside, fslab, own = call(
-        unpack_kernel,
-        (shape(2 * W, 2 * W), shape(2 * W, W), shape(2 * W, W)),
-        [SMEM, HBM, VMEM, VMEM],
-        (VMEM,) * 3,
-        [pltpu.VMEM((2 * ROWS, LANES), F32), dma],
-        0,
-        16 * block,
-    )(pos, l, slab, corner)
+        20 * block,
+        vmem=50,
+    )(pos, g, l, slab)
     gmine = after(gmine, fslab)
     sent = lax.ppermute(gmine, "col", [(14, 15)])
     gmine = tree_step(pos, gmine, 1, STEP_HINT)
@@ -418,12 +425,13 @@
     partial = call(
         sums_kernel, shape(16, 64, 2 * W), [SMEM] + [VMEM] * 4, VMEM, [], SUMS_HINT, 20 * block
     )(pos, gmine, gother, inside, chunk)
-    panels = exchange(after(partial, spread))
 
     sent = lax.ppermute(after(piece[:, W:], gmine), "col", [(15, 0)])
     smine = call(
         corner_kernel, shape(2 * W, W), [SMEM] + [VMEM] * 4, VMEM, [], CHAIN_HINT, 12 * block
     )(pos, after(spread, partial), own, sent, z)
+    panels = exchange(after(partial, smine))
+
     for step in range(3):
         smine = tree_step(pos, smine, step, LIGHT)
     sother = flipped(smine, "col", 1)
@@ -454,6 +462,9 @@
         below_kernel, shape(W, W), [SMEM] + [VMEM] * 3, VMEM, [], 4 * W**3, 8 * block
     )(pos, smine, sother, z)
     below_sent = lax.ppermute(below_row, "row", [(0, 15)])
+    ready = call(
+        ready_kernel, shape(W, 2 * W), [SMEM] + [VMEM] * 6, VMEM, [], LIGHT, LIGHT
+    )(pos, sums, panels, smine, sother, below_row, z)
     out = call(
         rows_kernel,
         shape(4 * ROWS, LANES),
@@ -464,7 +475,7 @@
         LIGHT,
         alias={9: 0},
         vmem=57,
-    )(pos, g, sums, panels, smine, sother, below_row, below_sent, z, out)
+    )(pos, g, ready, panels, smine, sother, below_row, below_sent, z, out)
     return out.reshape(adjoint.shape)
 
 

time: 143 us -> 143 us (level)
  starting transfers between devices: 48.2 us -> 46.7 us
    all_to_all x4, starting transfers between devices: 25.9 us -> 22.5 us  [exchange(): return lax.all_to_all(parts, 'row', 0, 0)]
    pallas_call x2 -> x3, Pallas kernels: 5.18 us -> 8.03 us  [the longest x1 2.8 us: per_device(): call(unpack_kernel, (shape(2 * W, 2 * W), shape(2 * W, W), shape(W, 2 * W...]
    ppermute x2, starting transfers between devices: 4.29 us -> 6.73 us  [flipped(): lax.ppermute(value, axis, [(i, i ^ flip) for i in range(lax.axis_size(axi...]
    unnamed x40 -> x44, local copies, waits for them, and re-layouts: 12.5 us -> 12.1 us
  transfers between devices with their start and end apart: 15 -> 15, of which waited for: 6 -> 8; matrix products, arithmetic and copies ran while one was open for 1% -> 0% of each run, Pallas kernels for 17% -> 18%
where the time goes in v3:
time: 143 us; the launch traced here: 141 us
  waiting for transfers between devices  46.9 us (33%)
  starting transfers between devices  46.7 us (33%)
  Pallas kernels  34.5 us (24%)
  local copies, waits for them, and re-layouts  12.1 us (8%)
    ppermute x6, waiting for transfers between devices, tree_step(): moved = lax.ppermute(value, 'col', pairs)  32.9 us
    all_to_all x4, starting transfers between devices, exchange(): return lax.all_to_all(parts, 'row', 0, 0)  22.5 us
    unnamed x44, local copies, waits for them, and re-layouts  12.1 us
    all_to_all x4, waiting for transfers between devices, exchange(): return lax.all_to_all(parts, 'row', 0, 0)  11.6 us
    ppermute x6, starting transfers between devices, tree_step(): moved = lax.ppermute(value, 'col', pairs)  9.42 us
    pallas_call x1, Pallas kernels, per_device(): call(bulk_kernel, shape(4 * ROWS, LANES), [SMEM, HBM] + [VMEM] * 6, HBM,...  8.21 us
    ppermute x1, starting transfers between devices, per_device(): below_sent = lax.ppermute(below_row, 'row', [(0, 15)])  6.78 us
    ppermute x2, starting transfers between devices, flipped(): lax.ppermute(value, axis, [(i, i ^ flip) for i in range(lax.axis_size(axi...  6.73 us
  transfers between devices with their start and end apart: 15, of which 8 were waited for; matrix products, arithmetic and copies ran while one was open for 0% of the time, Pallas kernels for 18%

profile of v3, /device:TPU:1, one launch (start us, length us, event | category | flops | bytes accessed | tf_op | source)
XLA Modules:
  0.0 141.0 jit_solution(10584937175499591623)
XLA Ops:
  0.0 2.5 %shard_map.37.kept.slab = f32[512,256]{1,0:T(8,128)} custom-call(f32[8192,128]{1,0:T(8,128)} %bitcast.8), custom_call_target="tpu_custom_call" | custom-call | bytes 2621440 | tf_op jit(solution)/shard_map/pallas_call | solution.py:377
  5.0 2.8 %shard_map.39 = (f32[512,512]{1,0:T(8,128)S(1)}, f32[512,256]{1,0:T(8,128)S(1)}, f32[256,512]{1,0:T(8,128)S(1)}, f32[512,256]{1,0:T(8,128)S(1)}) custom-call(s32[4]{0:T(128)S(1)} %pad_add_fusion.pos, f32[8192,128]{1,0:T(8,128)} %bitcast.9, f32[8192,128]{1,0:T(8,128)} %bitcast.12, f32[512,256]{1,0:T(8,128)S(1)} %copy-done.4), custom_call_target="tpu_custom_call" | custom-call | bytes 5242880 | tf_op jit(solution)/shard_map/pallas_call | solution.py:388
  7.8 9.2 %collective-permute-done.moved = f32[512,256]{1,0:T(8,128)S(1)} collective-permute-done((f32[512,256]{1,0:T(8,128)}, f32[512,256]{1,0:T(8,128)S(1)}, u32[]{:S(2)}, u32[]{:S(2)}) %collective-permute-start) | collective-permute-done | bytes 524320 | tf_op jit(solution)/shard_map/ppermute | solution.py:350
  17.0 1.4 shard_map.38.kept
  20.4 2.7 %shard_map.41 = f32[16,64,256]{2,1,0:T(8,128)} custom-call(s32[4]{0:T(128)S(1)} %pad_add_fusion.pos, f32[512,256]{1,0:T(8,128)S(1)} %collective-permute-done.2.sent, f32[512,256]{1,0:T(8,128)S(1)} %copy-done.4, f32[512,256]{1,0:T(8,128)S(1)} %get-tuple-element.18.fslab, f32[256,512]{1,0:T(8,128)S(1)} %get-tuple-element.20.piece), custom_call_target="tpu_custom_call" | custom-call | flops 134217728 | bytes 3145728 | tf_op jit(solution)/shard_map/pallas_call | solution.py:407
  23.1 6.8 %all-to-all-start = ((f32[16,64,256]{2,1,0:T(8,128)}), f32[16,64,256]{2,1,0:T(8,128)S(1)}, u32[]{:S(2)}, u32[]{:S(2)}) async-start(f32[16,64,256]{2,1,0:T(8,128)} %shard_map.41), calls=%async_computation | async-start | bytes 2097152 | tf_op jit(solution)/shard_map/all_to_all | solution.py:364
  33.3 2.1 %collective-permute-start.3 = (f32[512,256]{1,0:T(8,128)S(1)}, f32[512,256]{1,0:T(8,128)}, u32[]{:S(2)}, u32[]{:S(2)}) collective-permute-start(f32[512,256]{1,0:T(8,128)S(1)} %shard_map.40.kept), channel_id=1, source_target_pairs={{0,2},{14,12},{10,8},{4,6},{15,13},{1,3},{5,7},{11,9},{16,18},{30,... | collective-permute-start | bytes 1572872 | tf_op jit(solution)/shard_map/ppermute | solution.py:350
  35.4 9.3 %all-to-all-done.parts = f32[16,64,256]{2,1,0:T(8,128)S(1)} async-done(((f32[16,64,256]{2,1,0:T(8,128)}), f32[16,64,256]{2,1,0:T(8,128)S(1)}, u32[]{:S(2)}, u32[]{:S(2)}) %all-to-all-start) | async-done | bytes 1048608 | tf_op jit(solution)/shard_map/all_to_all | solution.py:364
  45.7 4.6 %all-to-all-start.1 = ((f32[16,24,512]{2,1,0:T(8,128)}), f32[16,24,512]{2,1,0:T(8,128)S(1)}, u32[]{:S(2)}, u32[]{:S(2)}) async-start(f32[16,24,512]{2,1,0:T(8,128)} %copy-done.15), calls=%async_computation.1 | async-start | bytes 1572864 | tf_op jit(solution)/shard_map/all_to_all | solution.py:364
  51.4 2.3 %collective-permute-start.4 = (f32[512,256]{1,0:T(8,128)S(1)}, f32[512,256]{1,0:T(8,128)S(1)}, u32[]{:S(2)}, u32[]{:S(2)}) collective-permute-start(f32[512,256]{1,0:T(8,128)S(1)} %shard_map.42.mine.gmine), channel_id=1, source_target_pairs={{0,1},{1,0},{2,3},{3,2},{4,5},{5,4},{6,7},{7,6},{8,9},{9,8},{10,11... | collective-permute-start | bytes 1572872 | tf_op jit(solution)/shard_map/ppermute | solution.py:356
  55.3 2.5 %shard_map.44 = f32[16,64,512]{2,1,0:T(8,128)S(1)} custom-call(s32[4]{0:T(128)S(1)} %pad_add_fusion.pos, f32[512,256]{1,0:T(8,128)S(1)} %shard_map.42.mine.gmine, f32[512,256]{1,0:T(8,128)S(1)} %collective-permute-done.4.other.gother, f32[512,512]{1,0:T(8,128)S(1)} %get-tuple-element.25.inside, f32[32,512]{1,0:T(8,128)S(1)} %get-tuple-element.26.chunk), custom_call_target="tpu_custom_call" | custom-call | flops 300000000 | bytes 5242880 | tf_op jit(solution)/shard_map/pallas_call | solution.py:425
  60.0 2.3 %all-to-all-done.1.parts = f32[16,24,512]{2,1,0:T(8,128)S(1)} async-done(((f32[16,24,512]{2,1,0:T(8,128)}), f32[16,24,512]{2,1,0:T(8,128)S(1)}, u32[]{:S(2)}, u32[]{:S(2)}) %all-to-all-start.1) | async-done | bytes 786464 | tf_op jit(solution)/shard_map/all_to_all | solution.py:364
  63.9 4.6 %all-to-all-start.2 = ((f32[16,64,512]{2,1,0:T(8,128)}), f32[16,64,512]{2,1,0:T(8,128)S(1)}, u32[]{:S(2)}, u32[]{:S(2)}) async-start(f32[16,64,512]{2,1,0:T(8,128)} %copy-done.5), calls=%async_computation.2 | async-start | bytes 4194304 | tf_op jit(solution)/shard_map/all_to_all | solution.py:364
  69.8 14.4 %collective-permute-done.6.moved = f32[512,256]{1,0:T(8,128)S(1)} collective-permute-done((f32[512,256]{1,0:T(8,128)S(1)}, f32[512,256]{1,0:T(8,128)S(1)}, u32[]{:S(2)}, u32[]{:S(2)}) %collective-permute-start.6) | collective-permute-done | bytes 524320 | tf_op jit(solution)/shard_map/ppermute | solution.py:350
  86.1 8.9 %collective-permute-done.7.moved = f32[512,256]{1,0:T(8,128)S(1)} collective-permute-done((f32[512,256]{1,0:T(8,128)S(1)}, f32[512,256]{1,0:T(8,128)S(1)}, u32[]{:S(2)}, u32[]{:S(2)}) %collective-permute-start.7) | collective-permute-done | bytes 524320 | tf_op jit(solution)/shard_map/ppermute | solution.py:350
  95.6 2.1 %collective-permute-start.8 = (f32[512,256]{1,0:T(8,128)S(1)}, f32[512,256]{1,0:T(8,128)}, u32[]{:S(2)}, u32[]{:S(2)}) collective-permute-start(f32[512,256]{1,0:T(8,128)S(1)} %shard_map.48.kept), channel_id=1, source_target_pairs={{0,2},{14,12},{10,8},{4,6},{15,13},{1,3},{5,7},{11,9},{16,18},{30,... | collective-permute-start | bytes 1572872 | tf_op jit(solution)/shard_map/ppermute | solution.py:350
  100.0 6.5 %all-to-all-start.3 = ((f32[16,32,512]{2,1,0:T(8,128)}), f32[16,32,512]{2,1,0:T(8,128)}, u32[]{:S(2)}, u32[]{:S(2)}) async-start(f32[16,32,512]{2,1,0:T(8,128)} %copy-done.14), calls=%async_computation.3 | async-start | bytes 2097152 | tf_op jit(solution)/shard_map/all_to_all | solution.py:364
  107.7 4.4 %collective-permute-start.9 = (f32[512,256]{1,0:T(8,128)S(1)}, f32[512,256]{1,0:T(8,128)S(1)}, u32[]{:S(2)}, u32[]{:S(2)}) collective-permute-start(f32[512,256]{1,0:T(8,128)S(1)} %shard_map.49.smine), channel_id=1, source_target_pairs={{0,1},{1,0},{2,3},{3,2},{4,5},{5,4},{6,7},{7,6},{8,9},{9,8},{10,11... | collective-permute-start | bytes 1572872 | tf_op jit(solution)/shard_map/ppermute | solution.py:356
  112.1 1.5 %collective-permute-done.9.sother = f32[512,256]{1,0:T(8,128)S(1)} collective-permute-done((f32[512,256]{1,0:T(8,128)S(1)}, f32[512,256]{1,0:T(8,128)S(1)}, u32[]{:S(2)}, u32[]{:S(2)}) %collective-permute-start.9) | collective-permute-done | bytes 524320 | tf_op jit(solution)/shard_map/ppermute | solution.py:356
  113.6 1.8 %shard_map.50.b_here = f32[256,256]{1,0:T(8,128)S(1)} custom-call(s32[4]{0:T(128)S(1)} %pad_add_fusion.pos, f32[512,256]{1,0:T(8,128)S(1)} %shard_map.49.smine, f32[512,256]{1,0:T(8,128)S(1)} %collective-permute-done.9.sother, f32[2,256,256]{2,1,0:T(8,128)S(1)} %copy-done.6), custom_call_target="tpu_custom_call" | custom-call | flops 67108864 | bytes 2097152 | tf_op jit(solution)/shard_map/pallas_call | solution.py:461
  115.4 6.8 %collective-permute-start.10 = (f32[256,256]{1,0:T(8,128)S(1)}, f32[256,256]{1,0:T(8,128)}, u32[]{:S(2)}, u32[]{:S(2)}) collective-permute-start(f32[256,256]{1,0:T(8,128)S(1)} %shard_map.50.b_here), channel_id=1, source_target_pairs={{0,240},{1,241},{2,242},{3,243},{4,244},{5,245},{6,246},{7,247},{8... | collective-permute-start | bytes 786440 | tf_op jit(solution)/shard_map/ppermute | solution.py:464
  122.2 8.2 %shard_map.52.done = f32[8192,128]{1,0:T(8,128)} custom-call(s32[4]{0:T(128)} %copy-done.16, f32[8192,128]{1,0:T(8,128)} %bitcast.10, f32[512,256]{1,0:T(8,128)} %copy-done.11, f32[512,256]{1,0:T(8,128)} %copy-done.12, f32[16,64,512]{2,1,0:T(8,128)} %copy-done, f32[512,256]{1,0:T(8,128)} %copy-done.2, f32[512,256]{1,0:T(8,128)} %copy-done.8, f32[2,256,256]{2,1,0:T(8,128)} %z.9), custom_call_target="tpu_custom_call" | custom-call | flops 503316480 | bytes 10485760 | tf_op jit(solution)/shard_map/pallas_call | solution.py:444
  132.6 2.7 %shard_map.51.ready = f32[256,512]{1,0:T(8,128)S(1)} custom-call(s32[4]{0:T(128)S(1)} %copy-done.17, f32[512,512]{1,0:T(8,128)} %bitcast.6.sums, f32[16,64,512]{2,1,0:T(8,128)S(1)} %copy-done.1, f32[512,256]{1,0:T(8,128)S(1)} %copy-done.3, f32[512,256]{1,0:T(8,128)S(1)} %copy-done.9, f32[256,256]{1,0:T(8,128)S(1)} %shard_map.50.b_here, ...), custom_call_target="tpu_custom_call" | custom-call | flops 1000 | bytes 1000 | tf_op jit(solution)/shard_map/pallas_call | solution.py:465
  136.1 4.7 %shard_map.53 = f32[8192,128]{1,0:T(8,128)} custom-call(s32[4]{0:T(128)} %copy-done.16, f32[8192,128]{1,0:T(8,128)} %bitcast.11, f32[256,512]{1,0:T(8,128)} %copy-done.13, f32[16,64,512]{2,1,0:T(8,128)} %copy-done, f32[512,256]{1,0:T(8,128)} %copy-done.2, f32[512,256]{1,0:T(8,128)} %copy-done.8, ...), custom_call_target="tpu_custom_call", output_to_operand_aliasing={{}: (9, {})} | custom-call | flops 1000 | bytes 1000 | tf_op jit(solution)/shard_map/pallas_call | solution.py:468
  (69 shorter events, 25.4 us)
Async XLA Ops:
  2.5 14.5 %collective-permute-start = (f32[512,256]{1,0:T(8,128)}, f32[512,256]{1,0:T(8,128)S(1)}, u32[]{:S(2)}, u32[]{:S(2)}) collective-permute-start(f32[512,256]{1,0:T(8,128)} %shard_map.37.kept.slab), channel_id=1, source_target_pairs={{0,14},{15,1},{16,30},{31,17},{32,46},{47,33},{48,62},{63,49},{64,... | collective-permute-start | bytes 1572872 | tf_op jit(solution)/shard_map/ppermute | solution.py:350
  3.9 109.7 %copy-start.16 = (s32[4]{0:T(128)}, s32[4]{0:T(128)S(1)}, u32[]{:S(2)}) copy-start(s32[4]{0:T(128)S(1)} %pad_add_fusion.pos) | copy-start | bytes 52
  7.8 15.3 %copy-start.18 = (f32[512,256]{1,0:T(8,128)}, f32[512,256]{1,0:T(8,128)S(1)}, u32[]{:S(2)}) copy-start(f32[512,256]{1,0:T(8,128)S(1)} %get-tuple-element.28.own) | copy-start | bytes 1572868
  18.4 2.0 %collective-permute-start.2 = (f32[512,256]{1,0:T(8,128)}, f32[512,256]{1,0:T(8,128)S(1)}, u32[]{:S(2)}, u32[]{:S(2)}) collective-permute-start(f32[512,256]{1,0:T(8,128)} %shard_map.38.kept), channel_id=1, source_target_pairs={{14,15},{30,31},{46,47},{62,63},{78,79},{94,95},{110,111},{126,127... | collective-permute-start | bytes 1572872 | tf_op jit(solution)/shard_map/ppermute | solution.py:404
  19.0 11.3 %collective-permute-start.1 = (f32[512,256]{1,0:T(8,128)}, f32[512,256]{1,0:T(8,128)S(1)}, u32[]{:S(2)}, u32[]{:S(2)}) collective-permute-start(f32[512,256]{1,0:T(8,128)} %shard_map.38.kept), channel_id=1, source_target_pairs={{0,4},{14,10},{15,11},{1,5},{16,20},{30,26},{31,27},{17,21},{32,36... | collective-permute-start | bytes 1572872 | tf_op jit(solution)/shard_map/ppermute | solution.py:350
  23.1 21.6 %all-to-all-start = ((f32[16,64,256]{2,1,0:T(8,128)}), f32[16,64,256]{2,1,0:T(8,128)S(1)}, u32[]{:S(2)}, u32[]{:S(2)}) async-start(f32[16,64,256]{2,1,0:T(8,128)} %shard_map.41), calls=%async_computation | async-start | bytes 2097152 | tf_op jit(solution)/shard_map/all_to_all | solution.py:364
  33.3 17.0 %collective-permute-start.3 = (f32[512,256]{1,0:T(8,128)S(1)}, f32[512,256]{1,0:T(8,128)}, u32[]{:S(2)}, u32[]{:S(2)}) collective-permute-start(f32[512,256]{1,0:T(8,128)S(1)} %shard_map.40.kept), channel_id=1, source_target_pairs={{0,2},{14,12},{10,8},{4,6},{15,13},{1,3},{5,7},{11,9},{16,18},{30,... | collective-permute-start | bytes 1572872 | tf_op jit(solution)/shard_map/ppermute | solution.py:350
  45.7 16.6 %all-to-all-start.1 = ((f32[16,24,512]{2,1,0:T(8,128)}), f32[16,24,512]{2,1,0:T(8,128)S(1)}, u32[]{:S(2)}, u32[]{:S(2)}) async-start(f32[16,24,512]{2,1,0:T(8,128)} %copy-done.15), calls=%async_computation.1 | async-start | bytes 1572864 | tf_op jit(solution)/shard_map/all_to_all | solution.py:364
  51.4 10.8 %copy-start.6 = (f32[2,256,256]{2,1,0:T(8,128)S(1)}, f32[2,256,256]{2,1,0:T(8,128)}, u32[]{:S(2)}) copy-start(f32[2,256,256]{2,1,0:T(8,128)} %z.9) | copy-start | bytes 1572868
  51.4 3.9 %collective-permute-start.4 = (f32[512,256]{1,0:T(8,128)S(1)}, f32[512,256]{1,0:T(8,128)S(1)}, u32[]{:S(2)}, u32[]{:S(2)}) collective-permute-start(f32[512,256]{1,0:T(8,128)S(1)} %shard_map.42.mine.gmine), channel_id=1, source_target_pairs={{0,1},{1,0},{2,3},{3,2},{4,5},{5,4},{6,7},{7,6},{8,9},{9,8},{10,11... | collective-permute-start | bytes 1572872 | tf_op jit(solution)/shard_map/ppermute | solution.py:356
  53.8 8.5 %collective-permute-start.5 = (f32[256,256]{1,0:T(8,128)S(1)}, f32[256,256]{1,0:T(8,128)S(1)}, u32[]{:S(2)}, u32[]{:S(2)}) collective-permute-start(f32[256,256]{1,0:T(8,128)S(1)} %slice.3), channel_id=1, source_target_pairs={{15,0},{31,16},{47,32},{63,48},{79,64},{95,80},{111,96},{127,112},... | collective-permute-start | bytes 786440 | tf_op jit(solution)/shard_map/ppermute | solution.py:429
  63.9 33.8 %all-to-all-start.2 = ((f32[16,64,512]{2,1,0:T(8,128)}), f32[16,64,512]{2,1,0:T(8,128)S(1)}, u32[]{:S(2)}, u32[]{:S(2)}) async-start(f32[16,64,512]{2,1,0:T(8,128)} %copy-done.5), calls=%async_computation.2 | async-start | bytes 4194304 | tf_op jit(solution)/shard_map/all_to_all | solution.py:364
  68.5 15.7 %collective-permute-start.6 = (f32[512,256]{1,0:T(8,128)S(1)}, f32[512,256]{1,0:T(8,128)S(1)}, u32[]{:S(2)}, u32[]{:S(2)}) collective-permute-start(f32[512,256]{1,0:T(8,128)S(1)} %shard_map.45.kept), channel_id=1, source_target_pairs={{0,14},{15,1},{16,30},{31,17},{32,46},{47,33},{48,62},{63,49},{64,... | collective-permute-start | bytes 1572872 | tf_op jit(solution)/shard_map/ppermute | solution.py:350
  84.8 10.2 %collective-permute-start.7 = (f32[512,256]{1,0:T(8,128)S(1)}, f32[512,256]{1,0:T(8,128)S(1)}, u32[]{:S(2)}, u32[]{:S(2)}) collective-permute-start(f32[512,256]{1,0:T(8,128)S(1)} %shard_map.47.kept), channel_id=1, source_target_pairs={{0,4},{14,10},{15,11},{1,5},{16,20},{30,26},{31,27},{17,21},{32,36... | collective-permute-start | bytes 1572872 | tf_op jit(solution)/shard_map/ppermute | solution.py:350
  95.6 11.0 %collective-permute-start.8 = (f32[512,256]{1,0:T(8,128)S(1)}, f32[512,256]{1,0:T(8,128)}, u32[]{:S(2)}, u32[]{:S(2)}) collective-permute-start(f32[512,256]{1,0:T(8,128)S(1)} %shard_map.48.kept), channel_id=1, source_target_pairs={{0,2},{14,12},{10,8},{4,6},{15,13},{1,3},{5,7},{11,9},{16,18},{30,... | collective-permute-start | bytes 1572872 | tf_op jit(solution)/shard_map/ppermute | solution.py:350
  100.0 30.4 %all-to-all-start.3 = ((f32[16,32,512]{2,1,0:T(8,128)}), f32[16,32,512]{2,1,0:T(8,128)}, u32[]{:S(2)}, u32[]{:S(2)}) async-start(f32[16,32,512]{2,1,0:T(8,128)} %copy-done.14), calls=%async_computation.3 | async-start | bytes 2097152 | tf_op jit(solution)/shard_map/all_to_all | solution.py:364
  107.7 14.5 %copy-start.2 = (f32[512,256]{1,0:T(8,128)}, f32[512,256]{1,0:T(8,128)S(1)}, u32[]{:S(2)}) copy-start(f32[512,256]{1,0:T(8,128)S(1)} %shard_map.49.smine) | copy-start | bytes 1572868
  107.7 5.9 %collective-permute-start.9 = (f32[512,256]{1,0:T(8,128)S(1)}, f32[512,256]{1,0:T(8,128)S(1)}, u32[]{:S(2)}, u32[]{:S(2)}) collective-permute-start(f32[512,256]{1,0:T(8,128)S(1)} %shard_map.49.smine), channel_id=1, source_target_pairs={{0,1},{1,0},{2,3},{3,2},{4,5},{5,4},{6,7},{7,6},{8,9},{9,8},{10,11... | collective-permute-start | bytes 1572872 | tf_op jit(solution)/shard_map/ppermute | solution.py:356
  113.6 8.6 %copy-start.8 = (f32[512,256]{1,0:T(8,128)}, f32[512,256]{1,0:T(8,128)S(1)}, u32[]{:S(2)}) copy-start(f32[512,256]{1,0:T(8,128)S(1)} %collective-permute-done.9.sother) | copy-start | bytes 1572868
  115.4 15.1 %copy-start.10 = (f32[256,256]{1,0:T(8,128)}, f32[256,256]{1,0:T(8,128)S(1)}, u32[]{:S(2)}) copy-start(f32[256,256]{1,0:T(8,128)S(1)} %shard_map.50.b_here) | copy-start | bytes 786436
  115.4 15.1 %copy-start.1 = (f32[16,64,512]{2,1,0:T(8,128)S(1)}, f32[16,64,512]{2,1,0:T(8,128)}, u32[]{:S(2)}) copy-start(f32[16,64,512]{2,1,0:T(8,128)} %copy-done) | copy-start | bytes 6291460
  115.4 15.1 %copy-start.7 = (f32[2,256,256]{2,1,0:T(8,128)S(1)}, f32[2,256,256]{2,1,0:T(8,128)}, u32[]{:S(2)}) copy-start(f32[2,256,256]{2,1,0:T(8,128)} %z.9) | copy-start | bytes 1572868
  115.4 15.1 %copy-start.17 = (s32[4]{0:T(128)S(1)}, s32[4]{0:T(128)}, u32[]{:S(2)}) copy-start(s32[4]{0:T(128)} %copy-done.16) | copy-start | bytes 52
  115.4 20.7 %collective-permute-start.10 = (f32[256,256]{1,0:T(8,128)S(1)}, f32[256,256]{1,0:T(8,128)}, u32[]{:S(2)}, u32[]{:S(2)}) collective-permute-start(f32[256,256]{1,0:T(8,128)S(1)} %shard_map.50.b_here), channel_id=1, source_target_pairs={{0,240},{1,241},{2,242},{3,243},{4,244},{5,245},{6,246},{7,247},{8... | collective-permute-start | bytes 786440 | tf_op jit(solution)/shard_map/ppermute | solution.py:464
  (13 other events, 16.1 us)

commit v4 on v3

--- a/solution.py
+++ b/solution.py
@@ -28,6 +28,16 @@
     return jnp.dot(left, right, precision=lax.Precision.HIGHEST, preferred_element_type=F32)
 
 
+def halves(value):
+    high = value.astype(jnp.bfloat16)
+    return high, (value - high.astype(F32)).astype(jnp.bfloat16)
+
+
+def wide(left, right):
+    (a, b), (c, d) = halves(left), halves(right)
+    return sum(jnp.dot(x, y, preferred_element_type=F32) for x, y in ((a, d), (b, c), (a, c)))
+
+
 def product_t(left, right):
     return lax.dot_general(
         left, right, (((0,), (0,)), ((), ())), precision=lax.Precision.HIGHEST, preferred_element_type=F32
@@ -205,7 +215,7 @@
     b0[...] = below0
     below1 = product(g31 - product(below0, l3231), z[1])
     b1[...] = below1
-    change = product(below0, panel_row(panels, 0)) + product(below1, panel_row(panels, 1))
+    change = wide(below0, panel_row(panels, 0)) + wide(below1, panel_row(panels, 1))
     above.wait()
     rest = pltpu.make_async_copy(abuf, out.at[pl.ds(0, 2 * ROWS)], sems.at[1])
     rest.start()

time: 143 us -> 142 us (level)
  transfers between devices with their start and end apart: 15 -> 15, of which waited for: 8 -> 8; matrix products, arithmetic and copies ran while one was open for 0% -> 0% of each run, Pallas kernels for 18% -> 17%
where the time goes in v4:
time: 142 us; the launch traced here: 140 us
  waiting for transfers between devices  46.9 us (33%)
  starting transfers between devices  46.7 us (33%)
  Pallas kernels  33.7 us (24%)
  local copies, waits for them, and re-layouts  12.1 us (9%)
    ppermute x6, waiting for transfers between devices, tree_step(): moved = lax.ppermute(value, 'col', pairs)  32.9 us
    all_to_all x4, starting transfers between devices, exchange(): return lax.all_to_all(parts, 'row', 0, 0)  22.5 us
    unnamed x44, local copies, waits for them, and re-layouts  12.1 us
    all_to_all x4, waiting for transfers between devices, exchange(): return lax.all_to_all(parts, 'row', 0, 0)  11.6 us
    ppermute x6, starting transfers between devices, tree_step(): moved = lax.ppermute(value, 'col', pairs)  9.42 us
    pallas_call x1, Pallas kernels, per_device(): call(bulk_kernel, shape(4 * ROWS, LANES), [SMEM, HBM] + [VMEM] * 6, HBM,...  7.38 us
    ppermute x1, starting transfers between devices, per_device(): below_sent = lax.ppermute(below_row, 'row', [(0, 15)])  6.78 us
    ppermute x2, starting transfers between devices, flipped(): lax.ppermute(value, axis, [(i, i ^ flip) for i in range(lax.axis_size(axi...  6.73 us
  transfers between devices with their start and end apart: 15, of which 8 were waited for; matrix products, arithmetic and copies ran while one was open for 0% of the time, Pallas kernels for 17%

profile of v4, /device:TPU:1, one launch (start us, length us, event | category | flops | bytes accessed | tf_op | source)
XLA Modules:
  0.0 140.2 jit_solution(8298488193985330273)
XLA Ops:
  0.0 2.5 %shard_map.37.kept.slab = f32[512,256]{1,0:T(8,128)} custom-call(f32[8192,128]{1,0:T(8,128)} %bitcast.8), custom_call_target="tpu_custom_call" | custom-call | bytes 2621440 | tf_op jit(solution)/shard_map/pallas_call | solution.py:387
  5.0 2.8 %shard_map.39 = (f32[512,512]{1,0:T(8,128)S(1)}, f32[512,256]{1,0:T(8,128)S(1)}, f32[256,512]{1,0:T(8,128)S(1)}, f32[512,256]{1,0:T(8,128)S(1)}) custom-call(s32[4]{0:T(128)S(1)} %pad_add_fusion.pos, f32[8192,128]{1,0:T(8,128)} %bitcast.9, f32[8192,128]{1,0:T(8,128)} %bitcast.12, f32[512,256]{1,0:T(8,128)S(1)} %copy-done.4), custom_call_target="tpu_custom_call" | custom-call | bytes 5242880 | tf_op jit(solution)/shard_map/pallas_call | solution.py:398
  7.8 9.2 %collective-permute-done.moved = f32[512,256]{1,0:T(8,128)S(1)} collective-permute-done((f32[512,256]{1,0:T(8,128)}, f32[512,256]{1,0:T(8,128)S(1)}, u32[]{:S(2)}, u32[]{:S(2)}) %collective-permute-start) | collective-permute-done | bytes 524320 | tf_op jit(solution)/shard_map/ppermute | solution.py:360
  17.0 1.4 shard_map.38.kept
  20.4 2.7 %shard_map.41 = f32[16,64,256]{2,1,0:T(8,128)} custom-call(s32[4]{0:T(128)S(1)} %pad_add_fusion.pos, f32[512,256]{1,0:T(8,128)S(1)} %collective-permute-done.2.sent, f32[512,256]{1,0:T(8,128)S(1)} %copy-done.4, f32[512,256]{1,0:T(8,128)S(1)} %get-tuple-element.18.fslab, f32[256,512]{1,0:T(8,128)S(1)} %get-tuple-element.20.piece), custom_call_target="tpu_custom_call" | custom-call | flops 134217728 | bytes 3145728 | tf_op jit(solution)/shard_map/pallas_call | solution.py:417
  23.1 6.8 %all-to-all-start = ((f32[16,64,256]{2,1,0:T(8,128)}), f32[16,64,256]{2,1,0:T(8,128)S(1)}, u32[]{:S(2)}, u32[]{:S(2)}) async-start(f32[16,64,256]{2,1,0:T(8,128)} %shard_map.41), calls=%async_computation | async-start | bytes 2097152 | tf_op jit(solution)/shard_map/all_to_all | solution.py:374
  33.3 2.1 %collective-permute-start.3 = (f32[512,256]{1,0:T(8,128)S(1)}, f32[512,256]{1,0:T(8,128)}, u32[]{:S(2)}, u32[]{:S(2)}) collective-permute-start(f32[512,256]{1,0:T(8,128)S(1)} %shard_map.40.kept), channel_id=1, source_target_pairs={{0,2},{14,12},{10,8},{4,6},{15,13},{1,3},{5,7},{11,9},{16,18},{30,... | collective-permute-start | bytes 1572872 | tf_op jit(solution)/shard_map/ppermute | solution.py:360
  35.4 9.3 %all-to-all-done.parts = f32[16,64,256]{2,1,0:T(8,128)S(1)} async-done(((f32[16,64,256]{2,1,0:T(8,128)}), f32[16,64,256]{2,1,0:T(8,128)S(1)}, u32[]{:S(2)}, u32[]{:S(2)}) %all-to-all-start) | async-done | bytes 1048608 | tf_op jit(solution)/shard_map/all_to_all | solution.py:374
  45.7 4.6 %all-to-all-start.1 = ((f32[16,24,512]{2,1,0:T(8,128)}), f32[16,24,512]{2,1,0:T(8,128)S(1)}, u32[]{:S(2)}, u32[]{:S(2)}) async-start(f32[16,24,512]{2,1,0:T(8,128)} %copy-done.15), calls=%async_computation.1 | async-start | bytes 1572864 | tf_op jit(solution)/shard_map/all_to_all | solution.py:374
  51.4 2.3 %collective-permute-start.4 = (f32[512,256]{1,0:T(8,128)S(1)}, f32[512,256]{1,0:T(8,128)S(1)}, u32[]{:S(2)}, u32[]{:S(2)}) collective-permute-start(f32[512,256]{1,0:T(8,128)S(1)} %shard_map.42.mine.gmine), channel_id=1, source_target_pairs={{0,1},{1,0},{2,3},{3,2},{4,5},{5,4},{6,7},{7,6},{8,9},{9,8},{10,11... | collective-permute-start | bytes 1572872 | tf_op jit(solution)/shard_map/ppermute | solution.py:366
  55.3 2.5 %shard_map.44 = f32[16,64,512]{2,1,0:T(8,128)S(1)} custom-call(s32[4]{0:T(128)S(1)} %pad_add_fusion.pos, f32[512,256]{1,0:T(8,128)S(1)} %shard_map.42.mine.gmine, f32[512,256]{1,0:T(8,128)S(1)} %collective-permute-done.4.other.gother, f32[512,512]{1,0:T(8,128)S(1)} %get-tuple-element.25.inside, f32[32,512]{1,0:T(8,128)S(1)} %get-tuple-element.26.chunk), custom_call_target="tpu_custom_call" | custom-call | flops 300000000 | bytes 5242880 | tf_op jit(solution)/shard_map/pallas_call | solution.py:435
  60.0 2.3 %all-to-all-done.1.parts = f32[16,24,512]{2,1,0:T(8,128)S(1)} async-done(((f32[16,24,512]{2,1,0:T(8,128)}), f32[16,24,512]{2,1,0:T(8,128)S(1)}, u32[]{:S(2)}, u32[]{:S(2)}) %all-to-all-start.1) | async-done | bytes 786464 | tf_op jit(solution)/shard_map/all_to_all | solution.py:374
  63.9 4.6 %all-to-all-start.2 = ((f32[16,64,512]{2,1,0:T(8,128)}), f32[16,64,512]{2,1,0:T(8,128)S(1)}, u32[]{:S(2)}, u32[]{:S(2)}) async-start(f32[16,64,512]{2,1,0:T(8,128)} %copy-done.5), calls=%async_computation.2 | async-start | bytes 4194304 | tf_op jit(solution)/shard_map/all_to_all | solution.py:374
  69.8 14.4 %collective-permute-done.6.moved = f32[512,256]{1,0:T(8,128)S(1)} collective-permute-done((f32[512,256]{1,0:T(8,128)S(1)}, f32[512,256]{1,0:T(8,128)S(1)}, u32[]{:S(2)}, u32[]{:S(2)}) %collective-permute-start.6) | collective-permute-done | bytes 524320 | tf_op jit(solution)/shard_map/ppermute | solution.py:360
  86.1 8.9 %collective-permute-done.7.moved = f32[512,256]{1,0:T(8,128)S(1)} collective-permute-done((f32[512,256]{1,0:T(8,128)S(1)}, f32[512,256]{1,0:T(8,128)S(1)}, u32[]{:S(2)}, u32[]{:S(2)}) %collective-permute-start.7) | collective-permute-done | bytes 524320 | tf_op jit(solution)/shard_map/ppermute | solution.py:360
  95.6 2.1 %collective-permute-start.8 = (f32[512,256]{1,0:T(8,128)S(1)}, f32[512,256]{1,0:T(8,128)}, u32[]{:S(2)}, u32[]{:S(2)}) collective-permute-start(f32[512,256]{1,0:T(8,128)S(1)} %shard_map.48.kept), channel_id=1, source_target_pairs={{0,2},{14,12},{10,8},{4,6},{15,13},{1,3},{5,7},{11,9},{16,18},{30,... | collective-permute-start | bytes 1572872 | tf_op jit(solution)/shard_map/ppermute | solution.py:360
  100.0 6.5 %all-to-all-start.3 = ((f32[16,32,512]{2,1,0:T(8,128)}), f32[16,32,512]{2,1,0:T(8,128)}, u32[]{:S(2)}, u32[]{:S(2)}) async-start(f32[16,32,512]{2,1,0:T(8,128)} %copy-done.14), calls=%async_computation.3 | async-start | bytes 2097152 | tf_op jit(solution)/shard_map/all_to_all | solution.py:374
  107.7 4.4 %collective-permute-start.9 = (f32[512,256]{1,0:T(8,128)S(1)}, f32[512,256]{1,0:T(8,128)S(1)}, u32[]{:S(2)}, u32[]{:S(2)}) collective-permute-start(f32[512,256]{1,0:T(8,128)S(1)} %shard_map.49.smine), channel_id=1, source_target_pairs={{0,1},{1,0},{2,3},{3,2},{4,5},{5,4},{6,7},{7,6},{8,9},{9,8},{10,11... | collective-permute-start | bytes 1572872 | tf_op jit(solution)/shard_map/ppermute | solution.py:366
  112.1 1.5 %collective-permute-done.9.sother = f32[512,256]{1,0:T(8,128)S(1)} collective-permute-done((f32[512,256]{1,0:T(8,128)S(1)}, f32[512,256]{1,0:T(8,128)S(1)}, u32[]{:S(2)}, u32[]{:S(2)}) %collective-permute-start.9) | collective-permute-done | bytes 524320 | tf_op jit(solution)/shard_map/ppermute | solution.py:366
  113.6 1.8 %shard_map.50.b_here = f32[256,256]{1,0:T(8,128)S(1)} custom-call(s32[4]{0:T(128)S(1)} %pad_add_fusion.pos, f32[512,256]{1,0:T(8,128)S(1)} %shard_map.49.smine, f32[512,256]{1,0:T(8,128)S(1)} %collective-permute-done.9.sother, f32[2,256,256]{2,1,0:T(8,128)S(1)} %copy-done.6), custom_call_target="tpu_custom_call" | custom-call | flops 67108864 | bytes 2097152 | tf_op jit(solution)/shard_map/pallas_call | solution.py:471
  115.4 6.8 %collective-permute-start.10 = (f32[256,256]{1,0:T(8,128)S(1)}, f32[256,256]{1,0:T(8,128)}, u32[]{:S(2)}, u32[]{:S(2)}) collective-permute-start(f32[256,256]{1,0:T(8,128)S(1)} %shard_map.50.b_here), channel_id=1, source_target_pairs={{0,240},{1,241},{2,242},{3,243},{4,244},{5,245},{6,246},{7,247},{8... | collective-permute-start | bytes 786440 | tf_op jit(solution)/shard_map/ppermute | solution.py:474
  122.2 7.4 %shard_map.52.done = f32[8192,128]{1,0:T(8,128)} custom-call(s32[4]{0:T(128)} %copy-done.16, f32[8192,128]{1,0:T(8,128)} %bitcast.10, f32[512,256]{1,0:T(8,128)} %copy-done.11, f32[512,256]{1,0:T(8,128)} %copy-done.12, f32[16,64,512]{2,1,0:T(8,128)} %copy-done, f32[512,256]{1,0:T(8,128)} %copy-done.2, f32[512,256]{1,0:T(8,128)} %copy-done.8, f32[2,256,256]{2,1,0:T(8,128)} %z.9), custom_call_target="tpu_custom_call" | custom-call | flops 503316480 | bytes 10485760 | tf_op jit(solution)/shard_map/pallas_call | solution.py:454
  131.7 2.7 %shard_map.51.ready = f32[256,512]{1,0:T(8,128)S(1)} custom-call(s32[4]{0:T(128)S(1)} %copy-done.17, f32[512,512]{1,0:T(8,128)} %bitcast.6.sums, f32[16,64,512]{2,1,0:T(8,128)S(1)} %copy-done.1, f32[512,256]{1,0:T(8,128)S(1)} %copy-done.3, f32[512,256]{1,0:T(8,128)S(1)} %copy-done.9, f32[256,256]{1,0:T(8,128)S(1)} %shard_map.50.b_here, ...), custom_call_target="tpu_custom_call" | custom-call | flops 1000 | bytes 1000 | tf_op jit(solution)/shard_map/pallas_call | solution.py:475
  135.3 4.7 %shard_map.53 = f32[8192,128]{1,0:T(8,128)} custom-call(s32[4]{0:T(128)} %copy-done.16, f32[8192,128]{1,0:T(8,128)} %bitcast.11, f32[256,512]{1,0:T(8,128)} %copy-done.13, f32[16,64,512]{2,1,0:T(8,128)} %copy-done, f32[512,256]{1,0:T(8,128)} %copy-done.2, f32[512,256]{1,0:T(8,128)} %copy-done.8, ...), custom_call_target="tpu_custom_call", output_to_operand_aliasing={{}: (9, {})} | custom-call | flops 1000 | bytes 1000 | tf_op jit(solution)/shard_map/pallas_call | solution.py:478
  (69 shorter events, 25.4 us)
Async XLA Ops:
  2.5 14.5 %collective-permute-start = (f32[512,256]{1,0:T(8,128)}, f32[512,256]{1,0:T(8,128)S(1)}, u32[]{:S(2)}, u32[]{:S(2)}) collective-permute-start(f32[512,256]{1,0:T(8,128)} %shard_map.37.kept.slab), channel_id=1, source_target_pairs={{0,14},{15,1},{16,30},{31,17},{32,46},{47,33},{48,62},{63,49},{64,... | collective-permute-start | bytes 1572872 | tf_op jit(solution)/shard_map/ppermute | solution.py:360
  3.9 109.7 %copy-start.16 = (s32[4]{0:T(128)}, s32[4]{0:T(128)S(1)}, u32[]{:S(2)}) copy-start(s32[4]{0:T(128)S(1)} %pad_add_fusion.pos) | copy-start | bytes 52
  7.8 15.3 %copy-start.18 = (f32[512,256]{1,0:T(8,128)}, f32[512,256]{1,0:T(8,128)S(1)}, u32[]{:S(2)}) copy-start(f32[512,256]{1,0:T(8,128)S(1)} %get-tuple-element.28.own) | copy-start | bytes 1572868
  18.4 2.0 %collective-permute-start.2 = (f32[512,256]{1,0:T(8,128)}, f32[512,256]{1,0:T(8,128)S(1)}, u32[]{:S(2)}, u32[]{:S(2)}) collective-permute-start(f32[512,256]{1,0:T(8,128)} %shard_map.38.kept), channel_id=1, source_target_pairs={{14,15},{30,31},{46,47},{62,63},{78,79},{94,95},{110,111},{126,127... | collective-permute-start | bytes 1572872 | tf_op jit(solution)/shard_map/ppermute | solution.py:414
  19.0 11.3 %collective-permute-start.1 = (f32[512,256]{1,0:T(8,128)}, f32[512,256]{1,0:T(8,128)S(1)}, u32[]{:S(2)}, u32[]{:S(2)}) collective-permute-start(f32[512,256]{1,0:T(8,128)} %shard_map.38.kept), channel_id=1, source_target_pairs={{0,4},{14,10},{15,11},{1,5},{16,20},{30,26},{31,27},{17,21},{32,36... | collective-permute-start | bytes 1572872 | tf_op jit(solution)/shard_map/ppermute | solution.py:360
  23.1 21.6 %all-to-all-start = ((f32[16,64,256]{2,1,0:T(8,128)}), f32[16,64,256]{2,1,0:T(8,128)S(1)}, u32[]{:S(2)}, u32[]{:S(2)}) async-start(f32[16,64,256]{2,1,0:T(8,128)} %shard_map.41), calls=%async_computation | async-start | bytes 2097152 | tf_op jit(solution)/shard_map/all_to_all | solution.py:374
  33.3 17.0 %collective-permute-start.3 = (f32[512,256]{1,0:T(8,128)S(1)}, f32[512,256]{1,0:T(8,128)}, u32[]{:S(2)}, u32[]{:S(2)}) collective-permute-start(f32[512,256]{1,0:T(8,128)S(1)} %shard_map.40.kept), channel_id=1, source_target_pairs={{0,2},{14,12},{10,8},{4,6},{15,13},{1,3},{5,7},{11,9},{16,18},{30,... | collective-permute-start | bytes 1572872 | tf_op jit(solution)/shard_map/ppermute | solution.py:360
  45.7 16.6 %all-to-all-start.1 = ((f32[16,24,512]{2,1,0:T(8,128)}), f32[16,24,512]{2,1,0:T(8,128)S(1)}, u32[]{:S(2)}, u32[]{:S(2)}) async-start(f32[16,24,512]{2,1,0:T(8,128)} %copy-done.15), calls=%async_computation.1 | async-start | bytes 1572864 | tf_op jit(solution)/shard_map/all_to_all | solution.py:374
  51.4 10.8 %copy-start.6 = (f32[2,256,256]{2,1,0:T(8,128)S(1)}, f32[2,256,256]{2,1,0:T(8,128)}, u32[]{:S(2)}) copy-start(f32[2,256,256]{2,1,0:T(8,128)} %z.9) | copy-start | bytes 1572868
  51.4 3.9 %collective-permute-start.4 = (f32[512,256]{1,0:T(8,128)S(1)}, f32[512,256]{1,0:T(8,128)S(1)}, u32[]{:S(2)}, u32[]{:S(2)}) collective-permute-start(f32[512,256]{1,0:T(8,128)S(1)} %shard_map.42.mine.gmine), channel_id=1, source_target_pairs={{0,1},{1,0},{2,3},{3,2},{4,5},{5,4},{6,7},{7,6},{8,9},{9,8},{10,11... | collective-permute-start | bytes 1572872 | tf_op jit(solution)/shard_map/ppermute | solution.py:366
  53.8 8.5 %collective-permute-start.5 = (f32[256,256]{1,0:T(8,128)S(1)}, f32[256,256]{1,0:T(8,128)S(1)}, u32[]{:S(2)}, u32[]{:S(2)}) collective-permute-start(f32[256,256]{1,0:T(8,128)S(1)} %slice.3), channel_id=1, source_target_pairs={{15,0},{31,16},{47,32},{63,48},{79,64},{95,80},{111,96},{127,112},... | collective-permute-start | bytes 786440 | tf_op jit(solution)/shard_map/ppermute | solution.py:439
  63.9 33.8 %all-to-all-start.2 = ((f32[16,64,512]{2,1,0:T(8,128)}), f32[16,64,512]{2,1,0:T(8,128)S(1)}, u32[]{:S(2)}, u32[]{:S(2)}) async-start(f32[16,64,512]{2,1,0:T(8,128)} %copy-done.5), calls=%async_computation.2 | async-start | bytes 4194304 | tf_op jit(solution)/shard_map/all_to_all | solution.py:374
  68.5 15.7 %collective-permute-start.6 = (f32[512,256]{1,0:T(8,128)S(1)}, f32[512,256]{1,0:T(8,128)S(1)}, u32[]{:S(2)}, u32[]{:S(2)}) collective-permute-start(f32[512,256]{1,0:T(8,128)S(1)} %shard_map.45.kept), channel_id=1, source_target_pairs={{0,14},{15,1},{16,30},{31,17},{32,46},{47,33},{48,62},{63,49},{64,... | collective-permute-start | bytes 1572872 | tf_op jit(solution)/shard_map/ppermute | solution.py:360
  84.8 10.2 %collective-permute-start.7 = (f32[512,256]{1,0:T(8,128)S(1)}, f32[512,256]{1,0:T(8,128)S(1)}, u32[]{:S(2)}, u32[]{:S(2)}) collective-permute-start(f32[512,256]{1,0:T(8,128)S(1)} %shard_map.47.kept), channel_id=1, source_target_pairs={{0,4},{14,10},{15,11},{1,5},{16,20},{30,26},{31,27},{17,21},{32,36... | collective-permute-start | bytes 1572872 | tf_op jit(solution)/shard_map/ppermute | solution.py:360
  95.6 11.0 %collective-permute-start.8 = (f32[512,256]{1,0:T(8,128)S(1)}, f32[512,256]{1,0:T(8,128)}, u32[]{:S(2)}, u32[]{:S(2)}) collective-permute-start(f32[512,256]{1,0:T(8,128)S(1)} %shard_map.48.kept), channel_id=1, source_target_pairs={{0,2},{14,12},{10,8},{4,6},{15,13},{1,3},{5,7},{11,9},{16,18},{30,... | collective-permute-start | bytes 1572872 | tf_op jit(solution)/shard_map/ppermute | solution.py:360
  100.0 29.6 %all-to-all-start.3 = ((f32[16,32,512]{2,1,0:T(8,128)}), f32[16,32,512]{2,1,0:T(8,128)}, u32[]{:S(2)}, u32[]{:S(2)}) async-start(f32[16,32,512]{2,1,0:T(8,128)} %copy-done.14), calls=%async_computation.3 | async-start | bytes 2097152 | tf_op jit(solution)/shard_map/all_to_all | solution.py:374
  107.7 14.5 %copy-start.2 = (f32[512,256]{1,0:T(8,128)}, f32[512,256]{1,0:T(8,128)S(1)}, u32[]{:S(2)}) copy-start(f32[512,256]{1,0:T(8,128)S(1)} %shard_map.49.smine) | copy-start | bytes 1572868
  107.7 5.9 %collective-permute-start.9 = (f32[512,256]{1,0:T(8,128)S(1)}, f32[512,256]{1,0:T(8,128)S(1)}, u32[]{:S(2)}, u32[]{:S(2)}) collective-permute-start(f32[512,256]{1,0:T(8,128)S(1)} %shard_map.49.smine), channel_id=1, source_target_pairs={{0,1},{1,0},{2,3},{3,2},{4,5},{5,4},{6,7},{7,6},{8,9},{9,8},{10,11... | collective-permute-start | bytes 1572872 | tf_op jit(solution)/shard_map/ppermute | solution.py:366
  113.6 8.6 %copy-start.8 = (f32[512,256]{1,0:T(8,128)}, f32[512,256]{1,0:T(8,128)S(1)}, u32[]{:S(2)}) copy-start(f32[512,256]{1,0:T(8,128)S(1)} %collective-permute-done.9.sother) | copy-start | bytes 1572868
  115.4 14.2 %copy-start.10 = (f32[256,256]{1,0:T(8,128)}, f32[256,256]{1,0:T(8,128)S(1)}, u32[]{:S(2)}) copy-start(f32[256,256]{1,0:T(8,128)S(1)} %shard_map.50.b_here) | copy-start | bytes 786436
  115.4 14.2 %copy-start.1 = (f32[16,64,512]{2,1,0:T(8,128)S(1)}, f32[16,64,512]{2,1,0:T(8,128)}, u32[]{:S(2)}) copy-start(f32[16,64,512]{2,1,0:T(8,128)} %copy-done) | copy-start | bytes 6291460
  115.4 14.2 %copy-start.7 = (f32[2,256,256]{2,1,0:T(8,128)S(1)}, f32[2,256,256]{2,1,0:T(8,128)}, u32[]{:S(2)}) copy-start(f32[2,256,256]{2,1,0:T(8,128)} %z.9) | copy-start | bytes 1572868
  115.4 14.2 %copy-start.17 = (s32[4]{0:T(128)S(1)}, s32[4]{0:T(128)}, u32[]{:S(2)}) copy-start(s32[4]{0:T(128)} %copy-done.16) | copy-start | bytes 52
  115.4 19.9 %collective-permute-start.10 = (f32[256,256]{1,0:T(8,128)S(1)}, f32[256,256]{1,0:T(8,128)}, u32[]{:S(2)}, u32[]{:S(2)}) collective-permute-start(f32[256,256]{1,0:T(8,128)S(1)} %shard_map.50.b_here), channel_id=1, source_target_pairs={{0,240},{1,241},{2,242},{3,243},{4,244},{5,245},{6,246},{7,247},{8... | collective-permute-start | bytes 786440 | tf_op jit(solution)/shard_map/ppermute | solution.py:474
  (13 other events, 16.1 us)
